TPU v7x, 512 devices: a whole 4x8x8 slice. The times are simulated.
512 devices in a mesh: island: 16 (over z, core), shard: 32 (over x, y).
Axes of the slice: x: 4, y: 8, z: 8, core: 2. Of those that a mesh axis runs over, the one named last changes fastest.
Arguments:
- island_deltas: bfloat16 [16, 12288, 4096], P('island', 'shard'), may hold values from -192 to 192
- start_basis: bfloat16 [4096, 128], P('shard'), may hold values from -6 to 6
- outer_params: float32 [12288, 4096], P('shard', 'island'), may hold values from -6 to 6
- momentum: float32 [12288, 4096], P('shard', 'island'), may hold values from -3 to 3
Outputs:
- new_params: float32 [12288, 4096], P('shard', 'island')
- new_momentum: float32 [12288, 4096], P('shard', 'island')
All inputs are finite; a program needn't handle non-finite values.
Results may differ from a plain program's by a relative error of at most 0.0013.
Values may be sent and summed in bfloat16 or wider, within the bound.
A program may use at most 64 MiB of HBM per device.

v0:
```python
import jax
import jax.numpy as jnp
from jax import lax
from jax.sharding import PartitionSpec as P

outer_rate = 0.7
outer_decay = 0.9


def body(island_deltas, start_basis, outer_params, momentum):
    local = island_deltas[0]
    islands = lax.axis_size("island")
    columns = local
    left_term = jnp.dot(
        columns,
        lax.all_gather(start_basis, "shard", axis=0, tiled=True),
        preferred_element_type=jnp.float32,
    )
    left = lax.psum(left_term, "island") / islands
    gram = lax.psum(jnp.dot(left.T, left, precision=lax.Precision.HIGHEST), "shard")
    factor = jnp.linalg.cholesky(gram)
    ortho = lax.linalg.triangular_solve(factor, left, left_side=False, lower=True, transpose_a=True)
    ortho_bf = ortho.astype(jnp.bfloat16)
    columns = local
    piece = (
        lax.psum_scatter(
            lax.dot_general(
                columns, ortho_bf, (((0,), (0,)), ((), ())), preferred_element_type=jnp.float32
            ),
            ("island", "shard"),
            scatter_dimension=0,
            tiled=True,
        )
        / islands
    )
    right = lax.all_gather(piece, "shard", axis=0, tiled=True)
    grad = jnp.dot(ortho, right.T, precision=lax.Precision.HIGHEST)
    new_momentum = outer_decay * momentum + grad
    new_params = outer_params - outer_rate * (grad + outer_decay * new_momentum)
    return (new_params, new_momentum)


def solution(mesh):
    placed = (
        P("island", "shard", None),
        P("shard", None),
        P("shard", "island"),
        P("shard", "island"),
    )
    return jax.shard_map(
        body,
        mesh=mesh,
        in_specs=placed,
        out_specs=(P("shard", "island"), P("shard", "island")),
        check_vma=False,
    )
```

profile of v0, /device:TPU:1, one launch (start us, length us, event | category | flops | bytes accessed | tf_op | source)
XLA Modules:
  0.0 709.8 jit_solution(8616111332221939964)
XLA Ops:
  7.2 0.0 all-gather.2.cloned.1.call-start
  7.2 0.7 all-gather.2.cloned.1.call-update
  7.9 0.0 all-reduce.5.cloned.1.call-start
  8.0 85.8 %all-gather.2.cloned.1.call-done = bf16[4096,128]{1,0:T(8,128)(2,1)} async-done(((bf16[128,128]{1,0:T(8,128)(2,1)}), bf16[4096,128]{1,0:T(8,128)(2,1)}) %all-gather.2.cloned.1.call-update) | async-done | bytes 1048592 | tf_op jit(solution)/shard_map/all_gather | solution.py:16
  93.7 2.9 fusion.1
  96.6 0.0 all-reduce.5.cloned.1.call-update
  96.6 0.0 all-reduce.7.cloned.1.call-start
  96.7 113.2 %all-reduce.5.cloned.1.call-done = f32[384,128]{1,0:T(8,128)} async-done(((f32[384,128]{1,0:T(8,128)}), f32[384,128]{1,0:T(8,128)}) %all-reduce.5.cloned.1.call-update) | async-done | bytes 196624 | tf_op jit(solution)/shard_map/psum | solution.py:19
  209.9 2.1 fusion.5
  212.0 0.0 all-reduce.9.cloned.1.call-start
  212.1 148.0 %all-reduce.7.cloned.1.call-done = f32[128,128]{0,1:T(8,128)} async-done(((f32[128,128]{0,1:T(8,128)}), f32[128,128]{0,1:T(8,128)}) %all-reduce.7.cloned.1.call-update) | async-done | bytes 65552 | tf_op jit(solution)/shard_map/psum | solution.py:20
  360.1 0.9 copy.12
  361.0 0.9 fusion.12
  361.9 11.7 %cholesky.16 = f32[128,128]{1,0:T(8,128)S(1)} custom-call(f32[128,128]{1,0:T(8,128)S(1)} %fusion.12), custom_call_target="Cholesky" | custom-call | tf_op jit(solution)/shard_map/jit(cholesky)/cholesky | solution.py:21
  373.6 0.6 compare_reduce_fusion
  374.3 0.7 fusion.10
  374.9 9.8 %custom-call.6 = f32[1,128,128]{1,2,0:T(8,128)S(1)} custom-call(f32[1,128,128]{2,1,0:T(8,128)S(1)} %fusion.10), custom_call_target="InvertDiagBlocksLowerTriangular" | custom-call | tf_op jit(solution)/shard_map/triangular_solve | solution.py:22
  384.7 1.2 fusion.3
  386.0 2.0 convolution_bitcast_fusion
  388.1 282.2 %all-reduce.9.cloned.1.call-done = f32[4096,128]{0,1:T(8,128)} async-done(((f32[4096,128]{0,1:T(8,128)}), f32[4096,128]{0,1:T(8,128)}) %all-reduce.9.cloned.1.call-update) | async-done | bytes 2097168
  670.2 0.9 constant_dynamic-slice_fusion
  671.2 0.1 copy.13
  671.2 29.5 %all_gather.7 = f32[256,128]{1,0:T(8,128)S(1)} all-gather(f32[8,128]{1,0:T(8,128)S(1)} %broadcast_multiply_fusion), channel_id=1, replica_groups=mesh['island'=16,'shard'=32] {'shard'}, dimensions={0}, use_global_device_ids=true | all-gather | bytes 135168 | tf_op jit(solution)/shard_map/all_gather | solution.py:36
  700.8 2.5 multiply_subtract_fusion
  (6 shorter events, 0.1 us)
Async XLA Ops:
  7.2 86.6 %copy-start = (bf16[1,384,4096]{2,1,0:T(8,128)(2,1)S(1)}, bf16[1,384,4096]{2,1,0:T(8,128)(2,1)}, u32[]{:S(2)}) copy-start(bf16[1,384,4096]{2,1,0:T(8,128)(2,1)} %param.4) | copy-start | bytes 9437188
  7.2 86.6 %all-gather.2.cloned.1.call-start = ((), (), s32[]{:S(2)}) async-start(), calls=%async_computation | async-start | bytes 1081344 | tf_op jit(solution)/shard_map/all_gather | solution.py:16
  7.9 201.9 %all-reduce.5.cloned.1.call-start = ((), (), s32[]{:S(2)}) async-start(), calls=%async_computation.1 | async-start | bytes 393216 | tf_op jit(solution)/shard_map/psum | solution.py:19
  96.6 263.4 %all-reduce.7.cloned.1.call-start = ((), (), s32[]{:S(2)}) async-start(), calls=%async_computation.2 | async-start | bytes 131072 | tf_op jit(solution)/shard_map/psum | solution.py:20
  212.0 458.2 %all-reduce.9.cloned.1.call-start = ((), (), s32[]{:S(2)}) async-start(), calls=%async_computation.3 | async-start | bytes 4194304
Sparse Core Ops, SparseCore 0:
  11.2 82.4 all-gather.1
  96.8 113.0 all-reduce.4
  214.3 145.7 all-reduce.6
  388.2 282.0 all-reduce.8
where the time goes:
time: 717 us; the launch traced here: 710 us
  waiting for transfers between devices  630 us (88%)
  blocking collectives  29.5 us (4%)
  other arithmetic  23.7 us (3%)
  between operations  13.8 us (2%)
  matrix products  10.8 us (2%)
    unnamed x5, waiting for transfers between devices  283 us
    psum x1, waiting for transfers between devices, body(): lax.psum(jnp.dot(left.T, left, precision=lax.Precision.HIGHEST), 'shard')  148 us
    psum x1, waiting for transfers between devices, body(): left = lax.psum(left_term, 'island') / islands  113 us
    all_gather x1, waiting for transfers between devices, body(): lax.all_gather(start_basis, 'shard', axis=0, tiled=True)  85.8 us
    all_gather x1, blocking collectives, body(): right = lax.all_gather(piece, 'shard', axis=0, tiled=True)  29.5 us
  transfers between devices with their start and end apart: 4, of which 4 were waited for; matrix products, arithmetic and copies ran while one was open for 0% of the time, Pallas kernels for 0%

commit v1 on v0

v1 whole, which is shorter than its diff:
```python
import functools

import jax
import jax.numpy as jnp
from jax import lax
from jax.experimental import pallas as pl
from jax.experimental.pallas import tpu as pltpu
from jax.sharding import PartitionSpec as P

outer_rate = 0.7
outer_decay = 0.9

MESH = pl.DeviceIdType.MESH
F32 = jnp.float32
BF16 = jnp.bfloat16
HIGHEST = lax.Precision.HIGHEST

NX, NY, NZ = 4, 8, 8
ROWS = 384
RANK = 128
HALF = ROWS // 2
PIECE = HALF // NZ
BLOCK = 256
SHARD = 128
SLICE = RANK // NX


def dot(a, b, precision=None):
    return jnp.dot(a, b, preferred_element_type=F32, precision=precision)


def invert_steps(a, steps):
    lane = lax.broadcasted_iota(jnp.int32, (8, RANK), 1)
    row = lax.broadcasted_iota(jnp.int32, (8, RANK), 0)

    def step(_, a):
        panel = a[0:8, :]
        columns = [jnp.broadcast_to(panel[:, j : j + 1], (8, RANK)) for j in range(8)]
        panel = jnp.where(lane < 8, (lane == row).astype(F32), panel)
        for j in range(8):
            here = row == j
            pivot = 1.0 / jnp.broadcast_to(columns[j][j : j + 1, :], (8, RANK))

            def reduced(values, j=j, here=here, pivot=pivot):
                scaled = jnp.broadcast_to(values[j : j + 1, :], (8, RANK)) * pivot
                return jnp.where(here, scaled, values - columns[j] * scaled)

            panel = reduced(panel)
            for m in range(j + 1, 8):
                columns[m] = reduced(columns[m])
        rest = a[8:, :]
        kept = jnp.where(lax.broadcasted_iota(jnp.int32, rest.shape, 1) < 8, 0.0, rest)
        for j in range(8):
            kept = kept - jnp.broadcast_to(rest[:, j : j + 1], rest.shape) * jnp.broadcast_to(
                panel[j : j + 1, :], rest.shape
            )
        return pltpu.roll(jnp.concatenate([kept, panel], axis=0), RANK - 8, 1)

    return lax.fori_loop(0, steps, step, a)


def kernel(
    deltas, basis, params, momentum,
    new_params, new_momentum,
    d_own, d_sib, s_all, l_part, l_sib, l_half, l_in, l_all,
    r_f32, r_b16, r_x, r_z, r_zin, r_y, r_yin, r_all,
    g_own, g_yin, g_x, g_xin, g_all, p_v, m_v, np_v, nm_v,
    local_sem,
    ds_s, ds_r, sy_s, sy_r, sx_s, sx_r, lc_s, lc_r, lz_s, lz_r, la_s, la_r, lf_s, lf_r,
    rx_s, rx_r, rz_s, rz_r, ry_s, ry_r, ra_s, ra_r, gy_s, gy_r, gx_s, gx_r, gc_s, gc_r,
):
    island = lax.axis_index("island")
    shard = lax.axis_index("shard")
    z, c = island // 2, lax.rem(island, 2)
    x, y = shard // NY, lax.rem(shard, NY)
    o = 1 - c

    def at_x(d):
        return (island, lax.rem(x + d, NX) * NY + y)

    def at_y(d):
        return (island, x * NY + lax.rem(y + d, NY))

    def at_z(d):
        return (lax.rem(z + d, NZ) * 2 + c, shard)

    sibling = (z * 2 + o, shard)
    sends = []

    def send(src, dst, s, r, device):
        copy = pltpu.make_async_remote_copy(
            src_ref=src, dst_ref=dst, send_sem=s, recv_sem=r, device_id=device, device_id_type=MESH
        )
        copy.start()
        sends.append(copy)

    def arrive(dst, s, r):
        pltpu.make_async_remote_copy(
            src_ref=dst, dst_ref=dst, send_sem=s, recv_sem=r, device_id=sibling, device_id_type=MESH
        ).wait_recv()

    barrier = pltpu.get_barrier_semaphore()
    partners = [at_y(d) for d in range(1, NY)] + [at_z(d) for d in range(1, NZ)] + [at_x(d) for d in range(1, NX)]
    for device in partners + [sibling]:
        pl.semaphore_signal(barrier, inc=1, device_id=device, device_id_type=MESH)

    loads = []
    for b in range(NZ):
        cols = pl.ds(pl.multiple_of((2 * b + c) * BLOCK, BLOCK), BLOCK)
        loads.append(pltpu.make_async_copy(deltas.at[0, :, cols], d_own.at[:, pl.ds(b * BLOCK, BLOCK)], local_sem.at[b]))
    state = [
        pltpu.make_async_copy(params, p_v, local_sem.at[NZ]),
        pltpu.make_async_copy(momentum, m_v, local_sem.at[NZ + 1]),
    ]
    for copy in loads + state:
        copy.start()

    pl.semaphore_wait(barrier, len(partners) + 1)

    mine = lax.rem(y // 2, 2) == c
    own_slot = 4 * x + 2 * (y // 4) + lax.rem(y, 2)

    def slot(index):
        return s_all.at[pl.ds(pl.multiple_of(index * SHARD, SHARD), SHARD)]

    def y_copies():
        own_k = own_slot - 4 * x
        return [
            pltpu.make_async_remote_copy(
                src_ref=basis, dst_ref=slot(own_slot), send_sem=sy_s.at[d], recv_sem=sy_r.at[own_k],
                device_id=at_y(d), device_id_type=MESH,
            )
            for d in range(1, NY)
        ]

    @pl.when(mine)
    def _():
        for copy in y_copies():
            copy.start()
        here = pltpu.make_async_copy(basis, slot(own_slot), local_sem.at[NZ + 2])
        here.start()
        here.wait()

    for b in range(NZ):
        cols = pl.ds(pl.multiple_of((2 * b + o) * BLOCK, BLOCK), BLOCK)
        send(deltas.at[0, :, cols], d_sib.at[:, pl.ds(b * BLOCK, BLOCK)], ds_s.at[b], ds_r.at[b], sibling)

    for k in range(4):
        source = (k % 2) + 2 * c + 4 * (k // 2)

        @pl.when(source != y)
        def _(k=k):
            arrive(slot(4 * x + k), sy_s.at[0], sy_r.at[k])

        for d in range(1, NX):
            send(slot(4 * x + k), slot(4 * x + k), sx_s.at[d, k], sx_r.at[d, k], at_x(d))
    for d in range(1, NX):
        for k in range(4):
            arrive(slot(4 * lax.rem(x + NX - d, NX) + k), sx_s.at[d, k], sx_r.at[d, k])
    for b in range(NZ):
        loads[b].wait()
        arrive(d_sib.at[:, pl.ds(b * BLOCK, BLOCK)], ds_s.at[b], ds_r.at[b])

    l_part[...] = dot(d_own[...], s_all[...]) + dot(d_sib[...], s_all[...])
    send(l_part.at[pl.ds(pl.multiple_of(HALF * o, HALF), HALF)], l_sib, lc_s.at[0], lc_r.at[0], sibling)
    arrive(l_sib, lc_s.at[0], lc_r.at[0])
    l_half[...] = l_part[pl.ds(pl.multiple_of(HALF * c, HALF), HALF), :] + l_sib[...]
    for d in range(1, NZ):
        rows = pl.ds(pl.multiple_of(PIECE * lax.rem(z + d, NZ), 8), PIECE)
        send(l_half.at[rows], l_in.at[d], lz_s.at[d], lz_r.at[d], at_z(d))
    total = l_half[pl.ds(pl.multiple_of(PIECE * z, 8), PIECE), :]
    for d in range(1, NZ):
        arrive(l_in.at[d], lz_s.at[d], lz_r.at[d])
        total = total + l_in[d]

    def piece(d):
        return pl.ds(pl.multiple_of(HALF * c + PIECE * lax.rem(z + NZ - d, NZ), 8), PIECE)

    def sibling_piece(d):
        return pl.ds(pl.multiple_of(HALF * o + PIECE * lax.rem(z + NZ - d, NZ), 8), PIECE)

    l_all[piece(0), :] = total
    for d in range(1, NZ):
        send(l_all.at[piece(0)], l_all.at[piece(0)], la_s.at[d], la_r.at[d], at_z(d))
    for d in range(NZ):
        if d:
            arrive(l_all.at[piece(d)], la_s.at[d], la_r.at[d])
        send(l_all.at[piece(d)], l_all.at[piece(d)], lf_s.at[d], lf_r.at[d], sibling)
    for d in range(NZ):
        arrive(l_all.at[sibling_piece(d)], lf_s.at[d], lf_r.at[d])

    left = l_all[...]
    left_t = left.T
    g_part = dot(left_t, left, HIGHEST)
    g_own[...] = jnp.where(c == 0, g_part[: RANK // 2], g_part[RANK // 2 :])
    for d in range(1, NY):
        send(g_own, g_yin.at[d], gy_s.at[d], gy_r.at[d], at_y(d))

    high = left_t.astype(BF16)
    low = (left_t - high.astype(F32)).astype(BF16)
    both = jnp.concatenate([high, low], axis=0)
    for b in range(NZ):
        cols = slice(b * BLOCK, (b + 1) * BLOCK)
        term = dot(both, d_own[:, cols]) + dot(both, d_sib[:, cols])
        term = term[:RANK] + term[RANK:]
        r_f32[b] = term
        r_b16[b] = term.astype(BF16)
        if b % 4 == 3:
            h = b // 4
            for d in range(1, NX):
                rank = pl.ds(pl.multiple_of(SLICE * lax.rem(x + d, NX), SLICE), SLICE)
                send(
                    r_b16.at[pl.ds(4 * h, 4), rank], r_x.at[d, pl.ds(4 * h, 4)],
                    rx_s.at[d, h], rx_r.at[d, h], at_x(d),
                )

    gram = g_own[...]
    for d in range(1, NY):
        arrive(g_yin.at[d], gy_s.at[d], gy_r.at[d])
        gram = gram + g_yin[d]
    g_x[...] = gram
    for d in range(1, NX):
        send(g_x, g_xin.at[d], gx_s.at[d], gx_r.at[d], at_x(d))

    rank_x = pl.ds(pl.multiple_of(SLICE * x, SLICE), SLICE)
    for h in range(2):
        for d in range(1, NX):
            arrive(r_x.at[d, pl.ds(4 * h, 4)], rx_s.at[d, h], rx_r.at[d, h])
        for b in range(4 * h, 4 * h + 4):
            term = r_f32[b, rank_x, :]
            for d in range(1, NX):
                term = term + r_x[d, b].astype(F32)
            r_z[b] = term
    for d in range(1, NZ):
        send(r_z.at[lax.rem(z + d, NZ)], r_zin.at[d], rz_s.at[d], rz_r.at[d], at_z(d))

    for d in range(1, NX):
        arrive(g_xin.at[d], gx_s.at[d], gx_r.at[d])
        gram = gram + g_xin[d]
    rows_c = pl.ds(pl.multiple_of(RANK // 2 * c, RANK // 2), RANK // 2)
    rows_o = pl.ds(pl.multiple_of(RANK // 2 * o, RANK // 2), RANK // 2)
    g_all[rows_c, :] = gram
    send(g_all.at[rows_c], g_all.at[rows_c], gc_s.at[0], gc_r.at[0], sibling)
    arrive(g_all.at[rows_o], gc_s.at[0], gc_r.at[0])
    inverse = invert_steps(g_all[...], 6)

    term = r_z[z]
    for d in range(1, NZ):
        arrive(r_zin.at[d], rz_s.at[d], rz_r.at[d])
        term = term + r_zin[d]
    r_y[...] = term
    for d in range(1, NY):
        send(r_y, r_yin.at[d], ry_s.at[d], ry_r.at[d], at_y(d))
    inverse = invert_steps(inverse, 10)
    ortho = dot(l_all[...], inverse, HIGHEST) * (1.0 / 16.0)
    for d in range(1, NY):
        arrive(r_yin.at[d], ry_s.at[d], ry_r.at[d])
        term = term + r_yin[d]
    r_all[rank_x, :] = term
    for d in range(1, NX):
        send(r_all.at[rank_x], r_all.at[rank_x], ra_s.at[d], ra_r.at[d], at_x(d))
    for copy in state:
        copy.wait()
    for d in range(1, NX):
        rank = pl.ds(pl.multiple_of(SLICE * lax.rem(x + NX - d, NX), SLICE), SLICE)
        arrive(r_all.at[rank], ra_s.at[d], ra_r.at[d])

    grad = dot(ortho, r_all[...], HIGHEST)
    updated = outer_decay * m_v[...] + grad
    nm_v[...] = updated
    np_v[...] = p_v[...] - outer_rate * (grad + outer_decay * updated)
    stores = [
        pltpu.make_async_copy(np_v, new_params, local_sem.at[NZ + 3]),
        pltpu.make_async_copy(nm_v, new_momentum, local_sem.at[NZ + 4]),
    ]
    for copy in stores:
        copy.start()
    for copy in sends:
        copy.wait_send()

    @pl.when(mine)
    def _():
        for copy in y_copies():
            copy.wait_send()

    for copy in stores:
        copy.wait()


def body(island_deltas, start_basis, outer_params, momentum):
    dma = pltpu.SemaphoreType.DMA
    vmem = pltpu.VMEM
    pair = lambda *shape: [dma(shape), dma(shape)]
    scratch = [
        vmem((ROWS, NZ * BLOCK), BF16),
        vmem((ROWS, NZ * BLOCK), BF16),
        vmem((NZ * BLOCK, RANK), BF16),
        vmem((ROWS, RANK), F32),
        vmem((HALF, RANK), F32),
        vmem((HALF, RANK), F32),
        vmem((NZ, PIECE, RANK), F32),
        vmem((ROWS, RANK), F32),
        vmem((NZ, RANK, BLOCK), F32),
        vmem((NZ, RANK, BLOCK), BF16),
        vmem((NX, NZ, SLICE, BLOCK), BF16),
        vmem((NZ, SLICE, BLOCK), F32),
        vmem((NZ, SLICE, BLOCK), F32),
        vmem((SLICE, BLOCK), F32),
        vmem((NY, SLICE, BLOCK), F32),
        vmem((RANK, BLOCK), F32),
        vmem((RANK // 2, RANK), F32),
        vmem((NY, RANK // 2, RANK), F32),
        vmem((RANK // 2, RANK), F32),
        vmem((NX, RANK // 2, RANK), F32),
        vmem((RANK, RANK), F32),
        vmem((ROWS, BLOCK), F32),
        vmem((ROWS, BLOCK), F32),
        vmem((ROWS, BLOCK), F32),
        vmem((ROWS, BLOCK), F32),
        dma((NZ + 5,)),
        *pair(NZ),
        dma((NY,)),
        dma((4,)),
        *pair(NX, 4),
        *pair(1),
        *pair(NZ),
        *pair(NZ),
        *pair(NZ),
        *pair(NX, 2),
        *pair(NZ),
        *pair(NY),
        *pair(NX),
        *pair(NY),
        *pair(NX),
        *pair(1),
    ]
    state = jax.ShapeDtypeStruct(outer_params.shape, F32)
    return tuple(
        pl.pallas_call(
            kernel,
            name="outer_step",
            out_shape=(state, state),
            in_specs=[pl.BlockSpec(memory_space=pl.ANY), pl.BlockSpec(memory_space=pltpu.VMEM)]
            + [pl.BlockSpec(memory_space=pl.ANY)] * 2,
            out_specs=(pl.BlockSpec(memory_space=pl.ANY),) * 2,
            scratch_shapes=scratch,
            compiler_params=pltpu.CompilerParams(
                collective_id=0, has_side_effects=True, vmem_limit_bytes=58 * 1024 * 1024
            ),
        )(island_deltas, start_basis, outer_params, momentum)
    )


def solution(mesh):
    placed = (
        P("island", "shard", None),
        P("shard", None),
        P("shard", "island"),
        P("shard", "island"),
    )
    return jax.shard_map(
        body,
        mesh=mesh,
        in_specs=placed,
        out_specs=(P("shard", "island"), P("shard", "island")),
        check_vma=False,
    )
```

time: 717 us -> 81.2 us (0.11)
  waiting for transfers between devices: 630 us -> 0 us
  Pallas kernels: 0 us -> 76.8 us
  blocking collectives: 29.5 us -> 0 us
  other arithmetic: 23.7 us -> 0 us
  between operations: 13.8 us -> 0.64 us
  matrix products: 10.8 us -> 0 us
    unnamed x5 -> x0, waiting for transfers between devices: 283 us -> none
    psum x2 -> x0, waiting for transfers between devices: 261 us -> none  [the longest x1 148 us: body(): lax.psum(jnp.dot(left.T, left, precision=lax.Precision.HIGHEST), 'shard')]
    all_gather x1 -> x0, waiting for transfers between devices: 85.8 us -> none  [body(): lax.all_gather(start_basis, 'shard', axis=0, tiled=True)]
    pallas_call x0 -> x1, Pallas kernels: none -> 76.8 us  [body(): pl.pallas_call(kernel, name='outer_step', out_shape=(state, state), in_sp...]
    all_gather x1 -> x0, blocking collectives: 29.5 us -> none  [body(): right = lax.all_gather(piece, 'shard', axis=0, tiled=True)]
    another operation x5 -> x0, other arithmetic: 22.9 us -> none  [the longest x3 12.4 us: body(): factor = jnp.linalg.cholesky(gram)]
    dot_general x4 -> x0, matrix products: 9.57 us -> none  [the longest x1 2.88 us: body(): jnp.dot(columns, lax.all_gather(start_basis, 'shard', axis=0, tiled=True)...]
  transfers between devices with their start and end apart: 4 -> 0, of which waited for: 4 -> 0; matrix products, arithmetic and copies ran while one was open for 0% -> 0% of each run, Pallas kernels for 0% -> 0%
where the time goes in v1:
time: 81.2 us; the launch traced here: 81 us
  Pallas kernels  76.8 us (95%)
  local copies, waits for them, and re-layouts  3.53 us (4%)
    pallas_call x1, Pallas kernels, body(): pl.pallas_call(kernel, name='outer_step', out_shape=(state, state), in_sp...  76.8 us
    unnamed x2, local copies, waits for them, and re-layouts  3.53 us

profile of v1, /device:TPU:1, one launch (start us, length us, event | category | flops | bytes accessed | tf_op | source)
XLA Modules:
  0.0 81.0 jit_solution(15882877967517967850)
XLA Ops:
  0.6 76.8 %outer_step.1 = (f32[384,256]{1,0:T(8,128)}, f32[384,256]{1,0:T(8,128)}) custom-call(bf16[1,384,4096]{2,1,0:T(8,128)(2,1)} %deltas.1, bf16[128,128]{1,0:T(8,128)(2,1)} %basis.1, f32[384,256]{1,0:T(8,128)} %params.1, f32[384,256]{1,0:T(8,128)} %momentum.1), custom_call_target="tpu_custom_call" | custom-call | tf_op jit(solution)/shard_map/outer_step/pallas_call | solution.py:339
  77.4 1.8 %copy.8 = f32[384,256]{1,0:T(8,128)} copy(f32[384,256]{1,0:T(8,128)} %get-tuple-element.4) | data formatting | bytes 786432
  79.2 1.8 %copy.9 = f32[384,256]{1,0:T(8,128)} copy(f32[384,256]{1,0:T(8,128)} %get-tuple-element.5) | data formatting | bytes 786432

commit v2 on v1

v2 whole, which is shorter than its diff:
```python
import functools

import jax
import jax.numpy as jnp
from jax import lax
from jax.experimental import pallas as pl
from jax.experimental.pallas import tpu as pltpu
from jax.sharding import PartitionSpec as P

outer_rate = 0.7
outer_decay = 0.9

MESH = pl.DeviceIdType.MESH
F32 = jnp.float32
BF16 = jnp.bfloat16
HIGHEST = lax.Precision.HIGHEST

NX, NY, NZ = 4, 8, 8
ROWS = 384
RANK = 128
HALF = ROWS // 2
PIECE = HALF // NZ
BLOCK = 256
SHARD = 128
SLICE = RANK // NX


AROUND_8 = (4, 3, 5, 2, 6, 1, 7)
AROUND_4 = (2, 1, 3)


def dot(a, b, precision=None):
    return jnp.dot(a, b, preferred_element_type=F32, precision=precision)


def invert_steps(a, steps):
    lane = lax.broadcasted_iota(jnp.int32, (8, RANK), 1)
    row = lax.broadcasted_iota(jnp.int32, (8, RANK), 0)

    def step(_, a):
        panel = a[0:8, :]
        columns = [jnp.broadcast_to(panel[:, j : j + 1], (8, RANK)) for j in range(8)]
        panel = jnp.where(lane < 8, (lane == row).astype(F32), panel)
        for j in range(8):
            here = row == j
            pivot = 1.0 / jnp.broadcast_to(columns[j][j : j + 1, :], (8, RANK))

            def reduced(values, j=j, here=here, pivot=pivot):
                scaled = jnp.broadcast_to(values[j : j + 1, :], (8, RANK)) * pivot
                return jnp.where(here, scaled, values - columns[j] * scaled)

            panel = reduced(panel)
            for m in range(j + 1, 8):
                columns[m] = reduced(columns[m])
        rest = a[8:, :]
        kept = jnp.where(lax.broadcasted_iota(jnp.int32, rest.shape, 1) < 8, 0.0, rest)
        for j in range(8):
            kept = kept - jnp.broadcast_to(rest[:, j : j + 1], rest.shape) * jnp.broadcast_to(
                panel[j : j + 1, :], rest.shape
            )
        return pltpu.roll(jnp.concatenate([kept, panel], axis=0), RANK - 8, 1)

    return lax.fori_loop(0, steps, step, a)


def kernel(
    deltas, basis, grad_out,
    d_own, d_sib, s_all, l_part, l_sib, l_half, l_in, l_all,
    a_f32, a_b16, a_x, a_z, a_zin, b_f32, b_b16, b_zin, b_x, b_xin, r_y, r_yin, r_all,
    g_own, g_yin, g_x, g_xin, g_all,
    local_sem,
    ds_s, ds_r, sy_s, sy_r, sx_s, sx_r, lc_s, lc_r, lz_s, lz_r, la_s, la_r, lf_s, lf_r,
    ax_s, ax_r, az_s, az_r, bz_s, bz_r, bx_s, bx_r, ry_s, ry_r, ra_s, ra_r, gy_s, gy_r, gx_s, gx_r, gc_s, gc_r,
):
    island = lax.axis_index("island")
    shard = lax.axis_index("shard")
    z, c = island // 2, lax.rem(island, 2)
    x, y = shard // NY, lax.rem(shard, NY)
    o = 1 - c

    def at_x(d):
        return (island, lax.rem(x + d, NX) * NY + y)

    def at_y(d):
        return (island, x * NY + lax.rem(y + d, NY))

    def at_z(d):
        return (lax.rem(z + d, NZ) * 2 + c, shard)

    sibling = (z * 2 + o, shard)
    sends = []

    def send(src, dst, s, r, device):
        copy = pltpu.make_async_remote_copy(
            src_ref=src, dst_ref=dst, send_sem=s, recv_sem=r, device_id=device, device_id_type=MESH
        )
        copy.start()
        sends.append(copy)

    def arrive(dst, s, r):
        pltpu.make_async_remote_copy(
            src_ref=dst, dst_ref=dst, send_sem=s, recv_sem=r, device_id=sibling, device_id_type=MESH
        ).wait_recv()

    barrier = pltpu.get_barrier_semaphore()
    partners = [at_y(d) for d in range(1, NY)] + [at_z(d) for d in range(1, NZ)] + [at_x(d) for d in range(1, NX)]
    for device in partners + [sibling]:
        pl.semaphore_signal(barrier, inc=1, device_id=device, device_id_type=MESH)

    loads = []
    for b in range(NZ):
        cols = pl.ds(pl.multiple_of((2 * b + c) * BLOCK, BLOCK), BLOCK)
        loads.append(pltpu.make_async_copy(deltas.at[0, :, cols], d_own.at[:, pl.ds(b * BLOCK, BLOCK)], local_sem.at[b]))
    for copy in loads:
        copy.start()

    pl.semaphore_wait(barrier, len(partners) + 1)

    mine = lax.rem(y // 2, 2) == c
    own_slot = 4 * x + 2 * (y // 4) + lax.rem(y, 2)

    def slot(index):
        return s_all.at[pl.ds(pl.multiple_of(index * SHARD, SHARD), SHARD)]

    def y_copies():
        own_k = own_slot - 4 * x
        return [
            pltpu.make_async_remote_copy(
                src_ref=basis, dst_ref=slot(own_slot), send_sem=sy_s.at[d], recv_sem=sy_r.at[own_k],
                device_id=at_y(d), device_id_type=MESH,
            )
            for d in AROUND_8
        ]

    @pl.when(mine)
    def _():
        for copy in y_copies():
            copy.start()
        here = pltpu.make_async_copy(basis, slot(own_slot), local_sem.at[NZ])
        here.start()
        here.wait()

    for b in range(NZ):
        cols = pl.ds(pl.multiple_of((2 * b + o) * BLOCK, BLOCK), BLOCK)
        send(deltas.at[0, :, cols], d_sib.at[:, pl.ds(b * BLOCK, BLOCK)], ds_s.at[b], ds_r.at[b], sibling)

    turn = 1 - 2 * lax.rem(y, 2)
    order = [jnp.where(mine, a, b) * turn for a, b in ((0, -1), (1, 2), (-3, -2), (4, 3))]
    for n, offset in enumerate(order):
        source = lax.rem(y + offset + NY, NY)
        k = lax.rem(source, 2) + 2 * (source // 4)
        if n == 0:

            @pl.when(jnp.logical_not(mine))
            def _():
                arrive(slot(4 * x + k), sy_s.at[0], sy_r.at[k])
        else:
            arrive(slot(4 * x + k), sy_s.at[0], sy_r.at[k])
        for d in AROUND_4:
            send(slot(4 * x + k), slot(4 * x + k), sx_s.at[d, n], sx_r.at[d, k], at_x(d))

    for b in range(NZ):
        loads[b].wait()
        arrive(d_sib.at[:, pl.ds(b * BLOCK, BLOCK)], ds_s.at[b], ds_r.at[b])

    def left_term(d):
        quarter = pl.ds(pl.multiple_of(4 * SHARD * lax.rem(x + NX - d, NX), 4 * SHARD), 4 * SHARD)
        return dot(d_own[:, quarter], s_all[quarter, :]) + dot(d_sib[:, quarter], s_all[quarter, :])

    l_part[...] = left_term(0)
    for d in (1, 3, 2):
        for k in range(4):
            arrive(slot(4 * lax.rem(x + NX - d, NX) + k), sx_s.at[d, k], sx_r.at[d, k])
        l_part[...] += left_term(d)
    send(l_part.at[pl.ds(pl.multiple_of(HALF * o, HALF), HALF)], l_sib, lc_s.at[0], lc_r.at[0], sibling)
    arrive(l_sib, lc_s.at[0], lc_r.at[0])
    l_half[...] = l_part[pl.ds(pl.multiple_of(HALF * c, HALF), HALF), :] + l_sib[...]
    for d in AROUND_8:
        rows = pl.ds(pl.multiple_of(PIECE * lax.rem(z + d, NZ), 8), PIECE)
        send(l_half.at[rows], l_in.at[d], lz_s.at[d], lz_r.at[d], at_z(d))
    total = l_half[pl.ds(pl.multiple_of(PIECE * z, 8), PIECE), :]
    for d in range(1, NZ):
        arrive(l_in.at[d], lz_s.at[d], lz_r.at[d])
        total = total + l_in[d]

    def piece(d):
        return pl.ds(pl.multiple_of(HALF * c + PIECE * lax.rem(z + NZ - d, NZ), 8), PIECE)

    def sibling_piece(d):
        return pl.ds(pl.multiple_of(HALF * o + PIECE * lax.rem(z + NZ - d, NZ), 8), PIECE)

    l_all[piece(0), :] = total
    for d in AROUND_8:
        send(l_all.at[piece(0)], l_all.at[piece(0)], la_s.at[d], la_r.at[d], at_z(d))
    for d in (0, *reversed(AROUND_8)):
        if d:
            arrive(l_all.at[piece(d)], la_s.at[d], la_r.at[d])
        send(l_all.at[piece(d)], l_all.at[piece(d)], lf_s.at[d], lf_r.at[d], sibling)
    for d in range(NZ):
        arrive(l_all.at[sibling_piece(d)], lf_s.at[d], lf_r.at[d])

    left = l_all[...]
    left_t = left.T
    high = left_t.astype(BF16)
    low = (left_t - high.astype(F32)).astype(BF16)
    both = jnp.concatenate([high, low], axis=0)

    def rank_of(d):
        return pl.ds(pl.multiple_of(SLICE * lax.rem(x + d, NX), SLICE), SLICE)

    for n, away in enumerate((*AROUND_8, 0)):
        cols = pl.ds(pl.multiple_of(BLOCK * lax.rem(z + away, NZ), BLOCK), BLOCK)
        term = dot(both, d_own[:, cols]) + dot(both, d_sib[:, cols])
        term = term[:RANK] + term[RANK:]
        a_f32[n] = term[:, :RANK]
        a_b16[n] = term[:, :RANK].astype(BF16)
        if away:
            b_b16[n] = term[:, RANK:].astype(BF16)
            send(b_b16.at[n], b_zin.at[n], bz_s.at[n], bz_r.at[n], at_z(away))
        else:
            b_f32[...] = term[:, RANK:]
        if n % 4 == 3:
            h = n // 4
            part = pl.ds(4 * h, 4)
            for d in AROUND_4:
                send(a_b16.at[part, rank_of(d)], a_x.at[d, part], ax_s.at[d, h], ax_r.at[d, h], at_x(d))

    g_part = dot(left_t, left, HIGHEST)
    g_own[...] = jnp.where(c == 0, g_part[: RANK // 2], g_part[RANK // 2 :])
    for d in AROUND_8:
        send(g_own, g_yin.at[d], gy_s.at[d], gy_r.at[d], at_y(d))

    for h in range(2):
        for d in range(1, NX):
            arrive(a_x.at[d, pl.ds(4 * h, 4)], ax_s.at[d, h], ax_r.at[d, h])
        for n in range(4 * h, 4 * h + 4):
            term = a_f32[n, rank_of(0), :]
            for d in range(1, NX):
                term = term + a_x[d, n].astype(F32)
            a_z[n] = term
            if n < NZ - 1:
                send(a_z.at[n], a_zin.at[n], az_s.at[n], az_r.at[n], at_z(AROUND_8[n]))

    b_sum = b_f32[...]
    for n in range(NZ - 1):
        arrive(b_zin.at[n], bz_s.at[n], bz_r.at[n])
        b_sum = b_sum + b_zin[n].astype(F32)
    b_x[...] = b_sum
    for d in AROUND_4:
        send(b_x.at[rank_of(d)], b_xin.at[d], bx_s.at[d], bx_r.at[d], at_x(d))

    gram = g_own[...]
    for d in range(1, NY):
        arrive(g_yin.at[d], gy_s.at[d], gy_r.at[d])
        gram = gram + g_yin[d]
    g_x[...] = gram
    for d in AROUND_4:
        send(g_x, g_xin.at[d], gx_s.at[d], gx_r.at[d], at_x(d))

    a_sum = a_z[NZ - 1]
    for n in range(NZ - 1):
        arrive(a_zin.at[n], az_s.at[n], az_r.at[n])
        a_sum = a_sum + a_zin[n]
    b_sum = b_x[rank_of(0), :]
    for d in range(1, NX):
        arrive(b_xin.at[d], bx_s.at[d], bx_r.at[d])
        b_sum = b_sum + b_xin[d]
    r_y[0] = a_sum
    r_y[1] = b_sum
    for d in AROUND_8:
        send(r_y, r_yin.at[d], ry_s.at[d], ry_r.at[d], at_y(d))

    for d in range(1, NX):
        arrive(g_xin.at[d], gx_s.at[d], gx_r.at[d])
        gram = gram + g_xin[d]
    rows_c = pl.ds(pl.multiple_of(RANK // 2 * c, RANK // 2), RANK // 2)
    rows_o = pl.ds(pl.multiple_of(RANK // 2 * o, RANK // 2), RANK // 2)
    g_all[rows_c, :] = gram
    send(g_all.at[rows_c], g_all.at[rows_c], gc_s.at[0], gc_r.at[0], sibling)
    arrive(g_all.at[rows_o], gc_s.at[0], gc_r.at[0])
    inverse = invert_steps(g_all[...], 10)

    term = r_y[...]
    for d in range(1, NY):
        arrive(r_yin.at[d], ry_s.at[d], ry_r.at[d])
        term = term + r_yin[d]
    r_all[:, rank_of(0), :] = term
    for d in AROUND_4:
        send(r_all.at[:, rank_of(0)], r_all.at[:, rank_of(0)], ra_s.at[d], ra_r.at[d], at_x(d))
    inverse = invert_steps(inverse, 6)
    ortho = dot(l_all[...], inverse, HIGHEST) * (1.0 / 16.0)
    for d in range(1, NX):
        arrive(r_all.at[:, rank_of(NX - d)], ra_s.at[d], ra_r.at[d])
    for h in range(2):
        grad_out[:, h * RANK : (h + 1) * RANK] = dot(ortho, r_all[h], HIGHEST)

    for copy in sends:
        copy.wait_send()

    @pl.when(mine)
    def _():
        for copy in y_copies():
            copy.wait_send()


def body(island_deltas, start_basis, outer_params, momentum):
    dma = pltpu.SemaphoreType.DMA
    vmem = pltpu.VMEM
    pair = lambda *shape: [dma(shape), dma(shape)]
    scratch = [
        vmem((ROWS, NZ * BLOCK), BF16),
        vmem((ROWS, NZ * BLOCK), BF16),
        vmem((NZ * BLOCK, RANK), BF16),
        vmem((ROWS, RANK), F32),
        vmem((HALF, RANK), F32),
        vmem((HALF, RANK), F32),
        vmem((NZ, PIECE, RANK), F32),
        vmem((ROWS, RANK), F32),
        vmem((NZ, RANK, RANK), F32),
        vmem((NZ, RANK, RANK), BF16),
        vmem((NX, NZ, SLICE, RANK), BF16),
        vmem((NZ, SLICE, RANK), F32),
        vmem((NZ, SLICE, RANK), F32),
        vmem((RANK, RANK), F32),
        vmem((NZ, RANK, RANK), BF16),
        vmem((NZ, RANK, RANK), BF16),
        vmem((RANK, RANK), F32),
        vmem((NX, SLICE, RANK), F32),
        vmem((2, SLICE, RANK), F32),
        vmem((NY, 2, SLICE, RANK), F32),
        vmem((2, RANK, RANK), F32),
        vmem((RANK // 2, RANK), F32),
        vmem((NY, RANK // 2, RANK), F32),
        vmem((RANK // 2, RANK), F32),
        vmem((NX, RANK // 2, RANK), F32),
        vmem((RANK, RANK), F32),
        dma((NZ + 1,)),
        *pair(NZ),
        dma((NY,)),
        dma((4,)),
        *pair(NX, 4),
        *pair(1),
        *pair(NZ),
        *pair(NZ),
        *pair(NZ),
        *pair(NX, 2),
        *pair(NZ),
        *pair(NZ),
        *pair(NX),
        *pair(NY),
        *pair(NX),
        *pair(NY),
        *pair(NX),
        *pair(1),
    ]
    grad = pl.pallas_call(
        kernel,
        name="outer_step",
        out_shape=jax.ShapeDtypeStruct(outer_params.shape, F32),
        in_specs=[pl.BlockSpec(memory_space=pltpu.HBM), pl.BlockSpec(memory_space=pltpu.VMEM)],
        out_specs=pl.BlockSpec(memory_space=pltpu.VMEM),
        scratch_shapes=scratch,
        compiler_params=pltpu.CompilerParams(
            collective_id=0, has_side_effects=True, vmem_limit_bytes=60 * 1024 * 1024
        ),
    )(island_deltas, start_basis)
    new_momentum = outer_decay * momentum + grad
    new_params = outer_params - outer_rate * (grad + outer_decay * new_momentum)
    return (new_params, new_momentum)


def solution(mesh):
    placed = (
        P("island", "shard", None),
        P("shard", None),
        P("shard", "island"),
        P("shard", "island"),
    )
    return jax.shard_map(
        body,
        mesh=mesh,
        in_specs=placed,
        out_specs=(P("shard", "island"), P("shard", "island")),
        check_vma=False,
    )
```

time: 81.2 us -> 69.8 us (0.86)
  Pallas kernels: 76.8 us -> 67 us
  local copies, waits for them, and re-layouts: 3.53 us -> 0.01 us
  other arithmetic: 0 us -> 1.97 us
    pallas_call x1, Pallas kernels: 76.8 us -> 67 us  [body(): pl.pallas_call(kernel, name='outer_step', out_shape=jax.ShapeDtypeStruct(...]
    unnamed x2 -> x4, local copies, waits for them, and re-layouts: 3.53 us -> 0.01 us
    sub x0 -> x1, other arithmetic: none -> 1.97 us  [body(): new_params = outer_params - outer_rate * (grad + outer_decay * new_momentum)]
where the time goes in v2:
time: 69.8 us; the launch traced here: 69.6 us
  Pallas kernels  67 us (96%)
  other arithmetic  1.97 us (3%)
    pallas_call x1, Pallas kernels, body(): pl.pallas_call(kernel, name='outer_step', out_shape=jax.ShapeDtypeStruct(...  67 us
    sub x1, other arithmetic, body(): new_params = outer_params - outer_rate * (grad + outer_decay * new_momentum)  1.97 us

profile of v2, /device:TPU:1, one launch (start us, length us, event | category | flops | bytes accessed | tf_op | source)
XLA Modules:
  0.0 69.6 jit_solution(6269822687310331206)
XLA Ops:
  0.6 0.0 copy-start.1
  0.6 0.0 copy-start
  0.7 67.0 %outer_step.1 = f32[384,256]{1,0:T(8,128)} custom-call(bf16[1,384,4096]{2,1,0:T(8,128)(2,1)} %deltas.1, bf16[128,128]{1,0:T(8,128)(2,1)} %basis.1), custom_call_target="tpu_custom_call" | custom-call | tf_op jit(solution)/shard_map/outer_step/pallas_call | solution.py:356
  67.6 0.0 copy-done.1
  67.7 0.0 copy-done
  67.7 2.0 %multiply_subtract_fusion = (f32[384,256]{1,0:T(8,128)}, f32[384,256]{1,0:T(8,128)}) fusion(f32[384,256]{1,0:T(8,128)S(1)} %copy-done, f32[384,256]{1,0:T(8,128)} %outer_step.1, f32[384,256]{1,0:T(8,128)S(1)} %copy-done.1), kind=kLoop, calls=%fused_computation | loop fusion | flops 589824 | bytes 1966080 | tf_op jit(solution)/shard_map/sub | solution.py:368
Async XLA Ops:
  0.6 67.0 %copy-start.1 = (f32[384,256]{1,0:T(8,128)S(1)}, f32[384,256]{1,0:T(8,128)}, u32[]{:S(2)}) copy-start(f32[384,256]{1,0:T(8,128)} %param.7) | copy-start | bytes 1179652
  0.6 67.0 %copy-start = (f32[384,256]{1,0:T(8,128)S(1)}, f32[384,256]{1,0:T(8,128)}, u32[]{:S(2)}) copy-start(f32[384,256]{1,0:T(8,128)} %param.6) | copy-start | bytes 1179652

commit v3 on v2

--- a/solution.py
+++ b/solution.py
@@ -64,9 +64,9 @@
 
 
 def kernel(
-    deltas, basis, grad_out,
-    d_own, d_sib, s_all, l_part, l_sib, l_half, l_in, l_all,
-    a_f32, a_b16, a_x, a_z, a_zin, b_f32, b_b16, b_zin, b_x, b_xin, r_y, r_yin, r_all,
+    deltas, basis, ortho_out, r_all,
+    basis_v, d_own, d_sib, s_all, l_part, l_sib, l_half, l_in, l_all,
+    a_f32, a_b16, a_x, a_z, a_zin, b_f32, b_b16, b_zin, b_x, b_xin, r_y, r_yin,
     g_own, g_yin, g_x, g_xin, g_all,
     local_sem,
     ds_s, ds_r, sy_s, sy_r, sx_s, sx_r, lc_s, lc_r, lz_s, lz_r, la_s, la_r, lf_s, lf_r,
@@ -107,6 +107,8 @@
     for device in partners + [sibling]:
         pl.semaphore_signal(barrier, inc=1, device_id=device, device_id_type=MESH)
 
+    basis_load = pltpu.make_async_copy(basis, basis_v, local_sem.at[NZ])
+    basis_load.start()
     loads = []
     for b in range(NZ):
         cols = pl.ds(pl.multiple_of((2 * b + c) * BLOCK, BLOCK), BLOCK)
@@ -114,6 +116,7 @@
     for copy in loads:
         copy.start()
 
+    basis_load.wait()
     pl.semaphore_wait(barrier, len(partners) + 1)
 
     mine = lax.rem(y // 2, 2) == c
@@ -126,7 +129,7 @@
         own_k = own_slot - 4 * x
         return [
             pltpu.make_async_remote_copy(
-                src_ref=basis, dst_ref=slot(own_slot), send_sem=sy_s.at[d], recv_sem=sy_r.at[own_k],
+                src_ref=basis_v, dst_ref=slot(own_slot), send_sem=sy_s.at[d], recv_sem=sy_r.at[own_k],
                 device_id=at_y(d), device_id_type=MESH,
             )
             for d in AROUND_8
@@ -136,9 +139,7 @@
     def _():
         for copy in y_copies():
             copy.start()
-        here = pltpu.make_async_copy(basis, slot(own_slot), local_sem.at[NZ])
-        here.start()
-        here.wait()
+        slot(own_slot)[...] = basis_v[...]
 
     for b in range(NZ):
         cols = pl.ds(pl.multiple_of((2 * b + o) * BLOCK, BLOCK), BLOCK)
@@ -288,12 +289,7 @@
     for d in AROUND_4:
         send(r_all.at[:, rank_of(0)], r_all.at[:, rank_of(0)], ra_s.at[d], ra_r.at[d], at_x(d))
     inverse = invert_steps(inverse, 6)
-    ortho = dot(l_all[...], inverse, HIGHEST) * (1.0 / 16.0)
-    for d in range(1, NX):
-        arrive(r_all.at[:, rank_of(NX - d)], ra_s.at[d], ra_r.at[d])
-    for h in range(2):
-        grad_out[:, h * RANK : (h + 1) * RANK] = dot(ortho, r_all[h], HIGHEST)
-
+    ortho_out[...] = dot(l_all[...], inverse, HIGHEST) * (1.0 / 16.0)
     for copy in sends:
         copy.wait_send()
 
@@ -301,6 +297,18 @@
     def _():
         for copy in y_copies():
             copy.wait_send()
+
+    for d in range(1, NX):
+        arrive(r_all.at[:, rank_of(NX - d)], ra_s.at[d], ra_r.at[d])
+
+
+def update(ortho, right, params, momentum, new_params, new_momentum):
+    for h in range(2):
+        cols = slice(h * RANK, (h + 1) * RANK)
+        grad = dot(ortho[...], right[h], HIGHEST)
+        updated = outer_decay * momentum[:, cols] + grad
+        new_momentum[:, cols] = updated
+        new_params[:, cols] = params[:, cols] - outer_rate * (grad + outer_decay * updated)
 
 
 def body(island_deltas, start_basis, outer_params, momentum):
@@ -308,6 +316,7 @@
     vmem = pltpu.VMEM
     pair = lambda *shape: [dma(shape), dma(shape)]
     scratch = [
+        vmem((SHARD, RANK), BF16),
         vmem((ROWS, NZ * BLOCK), BF16),
         vmem((ROWS, NZ * BLOCK), BF16),
         vmem((NZ * BLOCK, RANK), BF16),
@@ -328,7 +337,6 @@
         vmem((NX, SLICE, RANK), F32),
         vmem((2, SLICE, RANK), F32),
         vmem((NY, 2, SLICE, RANK), F32),
-        vmem((2, RANK, RANK), F32),
         vmem((RANK // 2, RANK), F32),
         vmem((NY, RANK // 2, RANK), F32),
         vmem((RANK // 2, RANK), F32),
@@ -353,20 +361,32 @@
         *pair(NX),
         *pair(1),
     ]
-    grad = pl.pallas_call(
+    in_vmem = pl.BlockSpec(memory_space=pltpu.VMEM)
+    ortho, right = pl.pallas_call(
         kernel,
-        name="outer_step",
-        out_shape=jax.ShapeDtypeStruct(outer_params.shape, F32),
-        in_specs=[pl.BlockSpec(memory_space=pltpu.HBM), pl.BlockSpec(memory_space=pltpu.VMEM)],
-        out_specs=pl.BlockSpec(memory_space=pltpu.VMEM),
+        name="factors",
+        out_shape=(jax.ShapeDtypeStruct((ROWS, RANK), F32), jax.ShapeDtypeStruct((2, RANK, RANK), F32)),
+        in_specs=[pl.BlockSpec(memory_space=pl.ANY)] * 2,
+        out_specs=(in_vmem, in_vmem),
         scratch_shapes=scratch,
         compiler_params=pltpu.CompilerParams(
-            collective_id=0, has_side_effects=True, vmem_limit_bytes=60 * 1024 * 1024
+            collective_id=0, has_side_effects=True, vmem_limit_bytes=24 * 1024 * 1024
         ),
-    )(island_deltas, start_basis)
-    new_momentum = outer_decay * momentum + grad
-    new_params = outer_params - outer_rate * (grad + outer_decay * new_momentum)
-    return (new_params, new_momentum)
+    )(
+        pltpu.with_memory_space_constraint(island_deltas, pltpu.HBM),
+        pltpu.with_memory_space_constraint(start_basis, pltpu.HBM),
+    )
+    state = jax.ShapeDtypeStruct(outer_params.shape, F32)
+    return tuple(
+        pl.pallas_call(
+            update,
+            name="update",
+            out_shape=(state, state),
+            in_specs=[in_vmem] * 4,
+            out_specs=(in_vmem, in_vmem),
+            compiler_params=pltpu.CompilerParams(vmem_limit_bytes=8 * 1024 * 1024),
+        )(ortho, right, outer_params, momentum)
+    )
 
 
 def solution(mesh):

time: 69.8 us -> 66.7 us (0.956)
  other arithmetic: 1.97 us -> 0 us
  Pallas kernels: 67 us -> 65.9 us
    sub x1 -> x0, other arithmetic: 1.97 us -> none  [body(): new_params = outer_params - outer_rate * (grad + outer_decay * new_momentum)]
    pallas_call x1 -> x2, Pallas kernels: 67 us -> 65.9 us  [the longest x1 64.5 us: body(): pl.pallas_call(kernel, name='factors', out_shape=(jax.ShapeDtypeStruct((R...]
where the time goes in v3:
time: 66.7 us; the launch traced here: 66.6 us
  Pallas kernels  65.9 us (99%)
  between operations  0.67 us (1%)
    pallas_call x1, Pallas kernels, body(): pl.pallas_call(kernel, name='factors', out_shape=(jax.ShapeDtypeStruct((R...  64.5 us
    pallas_call x1, Pallas kernels, body(): pl.pallas_call(update, name='update', out_shape=(state, state), in_specs=...  1.38 us

profile of v3, /device:TPU:1, one launch (start us, length us, event | category | flops | bytes accessed | tf_op | source)
XLA Modules:
  0.0 66.6 jit_solution(9439655471911655878)
XLA Ops:
  0.6 0.0 copy-start.1
  0.6 0.0 copy-start
  0.7 64.5 %factors.1 = (f32[384,128]{1,0:T(8,128)S(1)}, f32[2,128,128]{2,1,0:T(8,128)S(1)}) custom-call(bf16[1,384,4096]{2,1,0:T(8,128)(2,1)} %deltas.1, bf16[128,128]{1,0:T(8,128)(2,1)} %basis.1), custom_call_target="tpu_custom_call" | custom-call | tf_op jit(solution)/shard_map/factors/pallas_call | solution.py:365
  65.2 0.0 copy-done.1
  65.2 0.0 copy-done
  65.2 1.4 %update.1 = (f32[384,256]{1,0:T(8,128)}, f32[384,256]{1,0:T(8,128)}) custom-call(f32[384,128]{1,0:T(8,128)S(1)} %get-tuple-element.4.ortho, f32[2,128,128]{2,1,0:T(8,128)S(1)} %get-tuple-element.5.right, f32[384,256]{1,0:T(8,128)S(1)} %copy-done, f32[384,256]{1,0:T(8,128)S(1)} %copy-done.1), custom_call_target="tpu_custom_call" | custom-call | tf_op jit(solution)/shard_map/update/pallas_call | solution.py:381
Async XLA Ops:
  0.6 64.5 %copy-start.1 = (f32[384,256]{1,0:T(8,128)S(1)}, f32[384,256]{1,0:T(8,128)}, u32[]{:S(2)}) copy-start(f32[384,256]{1,0:T(8,128)} %momentum.1) | copy-start | bytes 1179652
  0.6 64.5 %copy-start = (f32[384,256]{1,0:T(8,128)S(1)}, f32[384,256]{1,0:T(8,128)}, u32[]{:S(2)}) copy-start(f32[384,256]{1,0:T(8,128)} %params.1) | copy-start | bytes 1179652

commit v4 on v3

--- a/solution.py
+++ b/solution.py
@@ -68,7 +68,7 @@
     basis_v, d_own, d_sib, s_all, l_part, l_sib, l_half, l_in, l_all,
     a_f32, a_b16, a_x, a_z, a_zin, b_f32, b_b16, b_zin, b_x, b_xin, r_y, r_yin,
     g_own, g_yin, g_x, g_xin, g_all,
-    local_sem,
+    load_sem, basis_sem,
     ds_s, ds_r, sy_s, sy_r, sx_s, sx_r, lc_s, lc_r, lz_s, lz_r, la_s, la_r, lf_s, lf_r,
     ax_s, ax_r, az_s, az_r, bz_s, bz_r, bx_s, bx_r, ry_s, ry_r, ra_s, ra_r, gy_s, gy_r, gx_s, gx_r, gc_s, gc_r,
 ):
@@ -88,33 +88,32 @@
         return (lax.rem(z + d, NZ) * 2 + c, shard)
 
     sibling = (z * 2 + o, shard)
-    sends = []
-
     def send(src, dst, s, r, device):
-        copy = pltpu.make_async_remote_copy(
+        pltpu.make_async_remote_copy(
             src_ref=src, dst_ref=dst, send_sem=s, recv_sem=r, device_id=device, device_id_type=MESH
+        ).start()
+
+    def whole_copy(whole, sem):
+        return pltpu.make_async_remote_copy(
+            src_ref=whole, dst_ref=whole, send_sem=sem, recv_sem=sem, device_id=sibling, device_id_type=MESH
         )
-        copy.start()
-        sends.append(copy)
-
-    def arrive(dst, s, r):
-        pltpu.make_async_remote_copy(
-            src_ref=dst, dst_ref=dst, send_sem=s, recv_sem=r, device_id=sibling, device_id_type=MESH
-        ).wait_recv()
+
+    def arrive(whole, r):
+        whole_copy(whole, r).wait_recv()
+
+    def sent(whole, s):
+        whole_copy(whole, s).wait_send()
 
     barrier = pltpu.get_barrier_semaphore()
     partners = [at_y(d) for d in range(1, NY)] + [at_z(d) for d in range(1, NZ)] + [at_x(d) for d in range(1, NX)]
     for device in partners + [sibling]:
         pl.semaphore_signal(barrier, inc=1, device_id=device, device_id_type=MESH)
 
-    basis_load = pltpu.make_async_copy(basis, basis_v, local_sem.at[NZ])
+    basis_load = pltpu.make_async_copy(basis, basis_v, basis_sem)
     basis_load.start()
-    loads = []
     for b in range(NZ):
         cols = pl.ds(pl.multiple_of((2 * b + c) * BLOCK, BLOCK), BLOCK)
-        loads.append(pltpu.make_async_copy(deltas.at[0, :, cols], d_own.at[:, pl.ds(b * BLOCK, BLOCK)], local_sem.at[b]))
-    for copy in loads:
-        copy.start()
+        pltpu.make_async_copy(deltas.at[0, :, cols], d_own.at[:, pl.ds(b * BLOCK, BLOCK)], load_sem).start()
 
     basis_load.wait()
     pl.semaphore_wait(barrier, len(partners) + 1)
@@ -125,25 +124,15 @@
     def slot(index):
         return s_all.at[pl.ds(pl.multiple_of(index * SHARD, SHARD), SHARD)]
 
-    def y_copies():
-        own_k = own_slot - 4 * x
-        return [
-            pltpu.make_async_remote_copy(
-                src_ref=basis_v, dst_ref=slot(own_slot), send_sem=sy_s.at[d], recv_sem=sy_r.at[own_k],
-                device_id=at_y(d), device_id_type=MESH,
-            )
-            for d in AROUND_8
-        ]
-
     @pl.when(mine)
     def _():
-        for copy in y_copies():
-            copy.start()
+        for d in AROUND_8:
+            send(basis_v, slot(own_slot), sy_s, sy_r.at[own_slot - 4 * x], at_y(d))
         slot(own_slot)[...] = basis_v[...]
 
     for b in range(NZ):
         cols = pl.ds(pl.multiple_of((2 * b + o) * BLOCK, BLOCK), BLOCK)
-        send(deltas.at[0, :, cols], d_sib.at[:, pl.ds(b * BLOCK, BLOCK)], ds_s.at[b], ds_r.at[b], sibling)
+        send(deltas.at[0, :, cols], d_sib.at[:, pl.ds(b * BLOCK, BLOCK)], ds_s, ds_r, sibling)
 
     turn = 1 - 2 * lax.rem(y, 2)
     order = [jnp.where(mine, a, b) * turn for a, b in ((0, -1), (1, 2), (-3, -2), (4, 3))]
@@ -154,51 +143,46 @@
 
             @pl.when(jnp.logical_not(mine))
             def _():
-                arrive(slot(4 * x + k), sy_s.at[0], sy_r.at[k])
+                arrive(slot(4 * x + k), sy_r.at[k])
         else:
-            arrive(slot(4 * x + k), sy_s.at[0], sy_r.at[k])
+            arrive(slot(4 * x + k), sy_r.at[k])
         for d in AROUND_4:
-            send(slot(4 * x + k), slot(4 * x + k), sx_s.at[d, n], sx_r.at[d, k], at_x(d))
-
-    for b in range(NZ):
-        loads[b].wait()
-        arrive(d_sib.at[:, pl.ds(b * BLOCK, BLOCK)], ds_s.at[b], ds_r.at[b])
+            send(slot(4 * x + k), slot(4 * x + k), sx_s, sx_r.at[d - 1], at_x(d))
+
+    pltpu.make_async_copy(d_own, d_own, load_sem).wait()
+    arrive(d_sib, ds_r)
+
+    def quarter(d):
+        return pl.ds(pl.multiple_of(4 * SHARD * lax.rem(x + NX - d, NX), 4 * SHARD), 4 * SHARD)
 
     def left_term(d):
-        quarter = pl.ds(pl.multiple_of(4 * SHARD * lax.rem(x + NX - d, NX), 4 * SHARD), 4 * SHARD)
-        return dot(d_own[:, quarter], s_all[quarter, :]) + dot(d_sib[:, quarter], s_all[quarter, :])
+        cols = quarter(d)
+        return dot(d_own[:, cols], s_all[cols, :]) + dot(d_sib[:, cols], s_all[cols, :])
 
     l_part[...] = left_term(0)
     for d in (1, 3, 2):
-        for k in range(4):
-            arrive(slot(4 * lax.rem(x + NX - d, NX) + k), sx_s.at[d, k], sx_r.at[d, k])
+        arrive(s_all.at[quarter(d)], sx_r.at[d - 1])
         l_part[...] += left_term(d)
-    send(l_part.at[pl.ds(pl.multiple_of(HALF * o, HALF), HALF)], l_sib, lc_s.at[0], lc_r.at[0], sibling)
-    arrive(l_sib, lc_s.at[0], lc_r.at[0])
+    send(l_part.at[pl.ds(pl.multiple_of(HALF * o, HALF), HALF)], l_sib, lc_s, lc_r, sibling)
+    arrive(l_sib, lc_r)
     l_half[...] = l_part[pl.ds(pl.multiple_of(HALF * c, HALF), HALF), :] + l_sib[...]
     for d in AROUND_8:
         rows = pl.ds(pl.multiple_of(PIECE * lax.rem(z + d, NZ), 8), PIECE)
-        send(l_half.at[rows], l_in.at[d], lz_s.at[d], lz_r.at[d], at_z(d))
+        send(l_half.at[rows], l_in.at[d], lz_s, lz_r, at_z(d))
     total = l_half[pl.ds(pl.multiple_of(PIECE * z, 8), PIECE), :]
+    arrive(l_in.at[pl.ds(1, NZ - 1)], lz_r)
     for d in range(1, NZ):
-        arrive(l_in.at[d], lz_s.at[d], lz_r.at[d])
         total = total + l_in[d]
 
-    def piece(d):
-        return pl.ds(pl.multiple_of(HALF * c + PIECE * lax.rem(z + NZ - d, NZ), 8), PIECE)
-
-    def sibling_piece(d):
-        return pl.ds(pl.multiple_of(HALF * o + PIECE * lax.rem(z + NZ - d, NZ), 8), PIECE)
-
-    l_all[piece(0), :] = total
+    own_half = l_all.at[pl.ds(pl.multiple_of(HALF * c, HALF), HALF)]
+    piece = l_all.at[pl.ds(pl.multiple_of(HALF * c + PIECE * z, 8), PIECE)]
+    piece[...] = total
+    others = l_half.at[pl.ds(0, HALF - PIECE)]
     for d in AROUND_8:
-        send(l_all.at[piece(0)], l_all.at[piece(0)], la_s.at[d], la_r.at[d], at_z(d))
-    for d in (0, *reversed(AROUND_8)):
-        if d:
-            arrive(l_all.at[piece(d)], la_s.at[d], la_r.at[d])
-        send(l_all.at[piece(d)], l_all.at[piece(d)], lf_s.at[d], lf_r.at[d], sibling)
-    for d in range(NZ):
-        arrive(l_all.at[sibling_piece(d)], lf_s.at[d], lf_r.at[d])
+        send(piece, piece, la_s, la_r, at_z(d))
+    arrive(others, la_r)
+    send(own_half, own_half, lf_s, lf_r, sibling)
+    arrive(l_half, lf_r)
 
     left = l_all[...]
     left_t = left.T
@@ -217,89 +201,99 @@
         a_b16[n] = term[:, :RANK].astype(BF16)
         if away:
             b_b16[n] = term[:, RANK:].astype(BF16)
-            send(b_b16.at[n], b_zin.at[n], bz_s.at[n], bz_r.at[n], at_z(away))
+            send(b_b16.at[n], b_zin.at[n], bz_s, bz_r, at_z(away))
         else:
             b_f32[...] = term[:, RANK:]
         if n % 4 == 3:
             h = n // 4
             part = pl.ds(4 * h, 4)
             for d in AROUND_4:
-                send(a_b16.at[part, rank_of(d)], a_x.at[d, part], ax_s.at[d, h], ax_r.at[d, h], at_x(d))
+                send(a_b16.at[part, rank_of(d)], a_x.at[d, part], ax_s, ax_r.at[h], at_x(d))
 
     g_part = dot(left_t, left, HIGHEST)
     g_own[...] = jnp.where(c == 0, g_part[: RANK // 2], g_part[RANK // 2 :])
     for d in AROUND_8:
-        send(g_own, g_yin.at[d], gy_s.at[d], gy_r.at[d], at_y(d))
+        send(g_own, g_yin.at[d], gy_s, gy_r, at_y(d))
 
     for h in range(2):
-        for d in range(1, NX):
-            arrive(a_x.at[d, pl.ds(4 * h, 4)], ax_s.at[d, h], ax_r.at[d, h])
+        arrive(a_x.at[pl.ds(1, NX - 1), pl.ds(4 * h, 4)], ax_r.at[h])
         for n in range(4 * h, 4 * h + 4):
             term = a_f32[n, rank_of(0), :]
             for d in range(1, NX):
                 term = term + a_x[d, n].astype(F32)
             a_z[n] = term
             if n < NZ - 1:
-                send(a_z.at[n], a_zin.at[n], az_s.at[n], az_r.at[n], at_z(AROUND_8[n]))
+                send(a_z.at[n], a_zin.at[n], az_s, az_r, at_z(AROUND_8[n]))
 
     b_sum = b_f32[...]
+    arrive(b_zin.at[pl.ds(0, NZ - 1)], bz_r)
     for n in range(NZ - 1):
-        arrive(b_zin.at[n], bz_s.at[n], bz_r.at[n])
         b_sum = b_sum + b_zin[n].astype(F32)
     b_x[...] = b_sum
     for d in AROUND_4:
-        send(b_x.at[rank_of(d)], b_xin.at[d], bx_s.at[d], bx_r.at[d], at_x(d))
+        send(b_x.at[rank_of(d)], b_xin.at[d], bx_s, bx_r, at_x(d))
 
     gram = g_own[...]
+    arrive(g_yin.at[pl.ds(1, NY - 1)], gy_r)
     for d in range(1, NY):
-        arrive(g_yin.at[d], gy_s.at[d], gy_r.at[d])
         gram = gram + g_yin[d]
     g_x[...] = gram
     for d in AROUND_4:
-        send(g_x, g_xin.at[d], gx_s.at[d], gx_r.at[d], at_x(d))
+        send(g_x, g_xin.at[d], gx_s, gx_r, at_x(d))
 
     a_sum = a_z[NZ - 1]
+    arrive(a_zin.at[pl.ds(0, NZ - 1)], az_r)
     for n in range(NZ - 1):
-        arrive(a_zin.at[n], az_s.at[n], az_r.at[n])
         a_sum = a_sum + a_zin[n]
     b_sum = b_x[rank_of(0), :]
+    arrive(b_xin.at[pl.ds(1, NX - 1)], bx_r)
     for d in range(1, NX):
-        arrive(b_xin.at[d], bx_s.at[d], bx_r.at[d])
         b_sum = b_sum + b_xin[d]
     r_y[0] = a_sum
     r_y[1] = b_sum
     for d in AROUND_8:
-        send(r_y, r_yin.at[d], ry_s.at[d], ry_r.at[d], at_y(d))
-
+        send(r_y, r_yin.at[d], ry_s, ry_r, at_y(d))
+
+    arrive(g_xin.at[pl.ds(1, NX - 1)], gx_r)
     for d in range(1, NX):
-        arrive(g_xin.at[d], gx_s.at[d], gx_r.at[d])
         gram = gram + g_xin[d]
     rows_c = pl.ds(pl.multiple_of(RANK // 2 * c, RANK // 2), RANK // 2)
     rows_o = pl.ds(pl.multiple_of(RANK // 2 * o, RANK // 2), RANK // 2)
     g_all[rows_c, :] = gram
-    send(g_all.at[rows_c], g_all.at[rows_c], gc_s.at[0], gc_r.at[0], sibling)
-    arrive(g_all.at[rows_o], gc_s.at[0], gc_r.at[0])
+    send(g_all.at[rows_c], g_all.at[rows_c], gc_s, gc_r, sibling)
+    arrive(g_all.at[rows_o], gc_r)
     inverse = invert_steps(g_all[...], 10)
 
     term = r_y[...]
+    arrive(r_yin.at[pl.ds(1, NY - 1)], ry_r)
     for d in range(1, NY):
-        arrive(r_yin.at[d], ry_s.at[d], ry_r.at[d])
         term = term + r_yin[d]
     r_all[:, rank_of(0), :] = term
     for d in AROUND_4:
-        send(r_all.at[:, rank_of(0)], r_all.at[:, rank_of(0)], ra_s.at[d], ra_r.at[d], at_x(d))
+        send(r_all.at[:, rank_of(0)], r_all.at[:, rank_of(0)], ra_s, ra_r, at_x(d))
     inverse = invert_steps(inverse, 6)
     ortho_out[...] = dot(l_all[...], inverse, HIGHEST) * (1.0 / 16.0)
-    for copy in sends:
-        copy.wait_send()
 
     @pl.when(mine)
     def _():
-        for copy in y_copies():
-            copy.wait_send()
-
-    for d in range(1, NX):
-        arrive(r_all.at[:, rank_of(NX - d)], ra_s.at[d], ra_r.at[d])
+        sent(s_all.at[pl.ds(0, (NY - 1) * SHARD)], sy_s)
+
+    sent(d_sib, ds_s)
+    sent(s_all.at[pl.ds(0, 4 * (NX - 1) * SHARD)], sx_s)
+    sent(l_half, lc_s)
+    sent(others, lz_s)
+    sent(others, la_s)
+    sent(l_half, lf_s)
+    sent(a_b16.at[pl.ds(0, 2 * (NX - 1))], ax_s)
+    sent(a_z.at[pl.ds(0, NZ - 1)], az_s)
+    sent(b_b16.at[pl.ds(0, NZ - 1)], bz_s)
+    sent(b_x.at[pl.ds(0, (NX - 1) * SLICE)], bx_s)
+    sent(r_yin.at[pl.ds(0, NY - 1)], ry_s)
+    sent(g_yin.at[pl.ds(0, NY - 1)], gy_s)
+    sent(g_xin.at[pl.ds(0, NX - 1)], gx_s)
+    sent(g_x, gc_s)
+    arrive(r_yin.at[pl.ds(0, NX - 1)], ra_r)
+    sent(r_yin.at[pl.ds(0, NX - 1)], ra_s)
 
 
 def update(ortho, right, params, momentum, new_params, new_momentum):
@@ -314,7 +308,6 @@
 def body(island_deltas, start_basis, outer_params, momentum):
     dma = pltpu.SemaphoreType.DMA
     vmem = pltpu.VMEM
-    pair = lambda *shape: [dma(shape), dma(shape)]
     scratch = [
         vmem((SHARD, RANK), BF16),
         vmem((ROWS, NZ * BLOCK), BF16),
@@ -342,24 +335,16 @@
         vmem((RANK // 2, RANK), F32),
         vmem((NX, RANK // 2, RANK), F32),
         vmem((RANK, RANK), F32),
-        dma((NZ + 1,)),
-        *pair(NZ),
-        dma((NY,)),
+        *[dma(())] * 2,
+        *[dma(())] * 2,
+        dma(()),
         dma((4,)),
-        *pair(NX, 4),
-        *pair(1),
-        *pair(NZ),
-        *pair(NZ),
-        *pair(NZ),
-        *pair(NX, 2),
-        *pair(NZ),
-        *pair(NZ),
-        *pair(NX),
-        *pair(NY),
-        *pair(NX),
-        *pair(NY),
-        *pair(NX),
-        *pair(1),
+        dma(()),
+        dma((NX - 1,)),
+        *[dma(())] * 8,
+        dma(()),
+        dma((2,)),
+        *[dma(())] * 16,
     ]
     in_vmem = pl.BlockSpec(memory_space=pltpu.VMEM)
     ortho, right = pl.pallas_call(

time: 66.7 us -> 65.2 us (0.978)
  Pallas kernels: 65.9 us -> 64.3 us
    pallas_call x1, Pallas kernels: 64.5 us -> 62.9 us  [body(): pl.pallas_call(kernel, name='factors', out_shape=(jax.ShapeDtypeStruct((R...]
where the time goes in v4:
time: 65.2 us; the launch traced here: 65 us
  Pallas kernels  64.3 us (99%)
  between operations  0.67 us (1%)
    pallas_call x1, Pallas kernels, body(): pl.pallas_call(kernel, name='factors', out_shape=(jax.ShapeDtypeStruct((R...  62.9 us
    pallas_call x1, Pallas kernels, body(): pl.pallas_call(update, name='update', out_shape=(state, state), in_specs=...  1.37 us

profile of v4, /device:TPU:1, one launch (start us, length us, event | category | flops | bytes accessed | tf_op | source)
XLA Modules:
  0.0 65.0 jit_solution(18043098759544040238)
XLA Ops:
  0.6 0.0 copy-start.1
  0.6 0.0 copy-start
  0.7 62.9 %factors.1 = (f32[384,128]{1,0:T(8,128)S(1)}, f32[2,128,128]{2,1,0:T(8,128)S(1)}) custom-call(bf16[1,384,4096]{2,1,0:T(8,128)(2,1)} %deltas.1, bf16[128,128]{1,0:T(8,128)(2,1)} %basis.1), custom_call_target="tpu_custom_call" | custom-call | tf_op jit(solution)/shard_map/factors/pallas_call | solution.py:350
  63.6 0.0 copy-done.1
  63.6 0.0 copy-done
  63.6 1.4 %update.1 = (f32[384,256]{1,0:T(8,128)}, f32[384,256]{1,0:T(8,128)}) custom-call(f32[384,128]{1,0:T(8,128)S(1)} %get-tuple-element.4.ortho, f32[2,128,128]{2,1,0:T(8,128)S(1)} %get-tuple-element.5.right, f32[384,256]{1,0:T(8,128)S(1)} %copy-done, f32[384,256]{1,0:T(8,128)S(1)} %copy-done.1), custom_call_target="tpu_custom_call" | custom-call | tf_op jit(solution)/shard_map/update/pallas_call | solution.py:366
Async XLA Ops:
  0.6 63.0 %copy-start.1 = (f32[384,256]{1,0:T(8,128)S(1)}, f32[384,256]{1,0:T(8,128)}, u32[]{:S(2)}) copy-start(f32[384,256]{1,0:T(8,128)} %momentum.1) | copy-start | bytes 1179652
  0.6 63.0 %copy-start = (f32[384,256]{1,0:T(8,128)S(1)}, f32[384,256]{1,0:T(8,128)}, u32[]{:S(2)}) copy-start(f32[384,256]{1,0:T(8,128)} %params.1) | copy-start | bytes 1179652

commit v5 on v4

--- a/solution.py
+++ b/solution.py
@@ -19,10 +19,12 @@
 ROWS = 384
 RANK = 128
 HALF = ROWS // 2
+STRIP = ROWS // 3
 PIECE = HALF // NZ
 BLOCK = 256
 SHARD = 128
 SLICE = RANK // NX
+PART = SLICE // 2
 
 
 AROUND_8 = (4, 3, 5, 2, 6, 1, 7)
@@ -67,7 +69,7 @@
     deltas, basis, ortho_out, r_all,
     basis_v, d_own, d_sib, s_all, l_part, l_sib, l_half, l_in, l_all,
     a_f32, a_b16, a_x, a_z, a_zin, b_f32, b_b16, b_zin, b_x, b_xin, r_y, r_yin,
-    g_own, g_yin, g_x, g_xin, g_all,
+    g_own, g_yin, g_xin, g_sum, g_all,
     load_sem, basis_sem,
     ds_s, ds_r, sy_s, sy_r, sx_s, sx_r, lc_s, lc_r, lz_s, lz_r, la_s, la_r, lf_s, lf_r,
     ax_s, ax_r, az_s, az_r, bz_s, bz_r, bx_s, bx_r, ry_s, ry_r, ra_s, ra_r, gy_s, gy_r, gx_s, gx_r, gc_s, gc_r,
@@ -126,7 +128,7 @@
 
     @pl.when(mine)
     def _():
-        for d in AROUND_8:
+        for d in (1, 7, 4, 2, 6, 3, 5):
             send(basis_v, slot(own_slot), sy_s, sy_r.at[own_slot - 4 * x], at_y(d))
         slot(own_slot)[...] = basis_v[...]
 
@@ -186,12 +188,24 @@
 
     left = l_all[...]
     left_t = left.T
+
+    g_part = dot(left_t, left, HIGHEST)
+    g_own[...] = jnp.where(c == 0, g_part[: RANK // 2], g_part[RANK // 2 :])
+    first, second = pl.ds(0, RANK // 4), pl.ds(RANK // 4, RANK // 4)
+    for d in AROUND_8:
+        send(g_own.at[first], g_yin.at[0, d], gy_s, gy_r.at[0], at_y(d))
+    for d in AROUND_4:
+        send(g_own.at[second], g_xin.at[1, d], gx_s, gx_r.at[1], at_x(d))
+
     high = left_t.astype(BF16)
     low = (left_t - high.astype(F32)).astype(BF16)
     both = jnp.concatenate([high, low], axis=0)
 
     def rank_of(d):
         return pl.ds(pl.multiple_of(SLICE * lax.rem(x + d, NX), SLICE), SLICE)
+
+    def send_b(n, q):
+        send(b_b16.at[q, n], b_zin.at[q, n], bz_s, bz_r.at[q], at_z(AROUND_8[n]))
 
     for n, away in enumerate((*AROUND_8, 0)):
         cols = pl.ds(pl.multiple_of(BLOCK * lax.rem(z + away, NZ), BLOCK), BLOCK)
@@ -199,79 +213,113 @@
         term = term[:RANK] + term[RANK:]
         a_f32[n] = term[:, :RANK]
         a_b16[n] = term[:, :RANK].astype(BF16)
+        for q in range(2):
+            for i in range(NX):
+                rows = slice(SLICE * i + PART * q, SLICE * i + PART * (q + 1))
+                if away:
+                    b_b16[q, n, i] = term[rows, RANK:].astype(BF16)
+                else:
+                    b_f32[q, i] = term[rows, RANK:]
         if away:
-            b_b16[n] = term[:, RANK:].astype(BF16)
-            send(b_b16.at[n], b_zin.at[n], bz_s, bz_r, at_z(away))
-        else:
-            b_f32[...] = term[:, RANK:]
+            send_b(n, 0)
         if n % 4 == 3:
             h = n // 4
             part = pl.ds(4 * h, 4)
             for d in AROUND_4:
                 send(a_b16.at[part, rank_of(d)], a_x.at[d, part], ax_s, ax_r.at[h], at_x(d))
-
-    g_part = dot(left_t, left, HIGHEST)
-    g_own[...] = jnp.where(c == 0, g_part[: RANK // 2], g_part[RANK // 2 :])
+    for n in range(NZ - 1):
+        send_b(n, 1)
+
+    others_x, others_y, others_z = pl.ds(1, NX - 1), pl.ds(1, NY - 1), pl.ds(0, NZ - 1)
+    arrive(g_xin.at[1, others_x], gx_r.at[1])
+    g_second = g_own[second, :]
+    for d in range(1, NX):
+        g_second = g_second + g_xin[1, d]
+    g_sum[1] = g_second
     for d in AROUND_8:
-        send(g_own, g_yin.at[d], gy_s, gy_r, at_y(d))
+        send(g_sum.at[1], g_yin.at[1, d], gy_s, gy_r.at[1], at_y(d))
+
+    def send_a(n, q):
+        send(a_z.at[q, n], a_zin.at[q, n], az_s, az_r.at[q], at_z(AROUND_8[n]))
 
     for h in range(2):
-        arrive(a_x.at[pl.ds(1, NX - 1), pl.ds(4 * h, 4)], ax_r.at[h])
+        arrive(a_x.at[others_x, pl.ds(4 * h, 4)], ax_r.at[h])
         for n in range(4 * h, 4 * h + 4):
             term = a_f32[n, rank_of(0), :]
             for d in range(1, NX):
                 term = term + a_x[d, n].astype(F32)
-            a_z[n] = term
+            a_z[0, n] = term[:PART]
+            a_z[1, n] = term[PART:]
             if n < NZ - 1:
-                send(a_z.at[n], a_zin.at[n], az_s, az_r, at_z(AROUND_8[n]))
-
-    b_sum = b_f32[...]
-    arrive(b_zin.at[pl.ds(0, NZ - 1)], bz_r)
+                send_a(n, 0)
     for n in range(NZ - 1):
-        b_sum = b_sum + b_zin[n].astype(F32)
-    b_x[...] = b_sum
+        send_a(n, 1)
+
+    def sum_b(q):
+        arrive(b_zin.at[q, others_z], bz_r.at[q])
+        total = b_f32[q]
+        for n in range(NZ - 1):
+            total = total + b_zin[q, n].astype(F32)
+        b_x[q] = total
+        for d in AROUND_4:
+            send(b_x.at[q, lax.rem(x + d, NX)], b_xin.at[q, d], bx_s, bx_r.at[q], at_x(d))
+
+    def send_y(u):
+        for d in AROUND_8:
+            send(r_y.at[u], r_yin.at[u, d], ry_s, ry_r.at[u], at_y(d))
+
+    def end_a(q):
+        arrive(a_zin.at[q, others_z], az_r.at[q])
+        total = a_z[q, NZ - 1]
+        for n in range(NZ - 1):
+            total = total + a_zin[q, n]
+        r_y[q] = total
+        send_y(q)
+
+    def end_b(q):
+        arrive(b_xin.at[q, others_x], bx_r.at[q])
+        total = b_x[q, x]
+        for d in range(1, NX):
+            total = total + b_xin[q, d]
+        r_y[2 + q] = total
+        send_y(2 + q)
+
+    sum_b(0)
+    arrive(g_yin.at[0, others_y], gy_r.at[0])
+    g_first = g_own[first, :]
+    for d in range(1, NY):
+        g_first = g_first + g_yin[0, d]
+    g_sum[0] = g_first
     for d in AROUND_4:
-        send(b_x.at[rank_of(d)], b_xin.at[d], bx_s, bx_r, at_x(d))
-
-    gram = g_own[...]
-    arrive(g_yin.at[pl.ds(1, NY - 1)], gy_r)
+        send(g_sum.at[0], g_xin.at[0, d], gx_s, gx_r.at[0], at_x(d))
+    sum_b(1)
+    end_b(0)
+    arrive(g_xin.at[0, others_x], gx_r.at[0])
+    for d in range(1, NX):
+        g_first = g_first + g_xin[0, d]
+    arrive(g_yin.at[1, others_y], gy_r.at[1])
     for d in range(1, NY):
-        gram = gram + g_yin[d]
-    g_x[...] = gram
-    for d in AROUND_4:
-        send(g_x, g_xin.at[d], gx_s, gx_r, at_x(d))
-
-    a_sum = a_z[NZ - 1]
-    arrive(a_zin.at[pl.ds(0, NZ - 1)], az_r)
-    for n in range(NZ - 1):
-        a_sum = a_sum + a_zin[n]
-    b_sum = b_x[rank_of(0), :]
-    arrive(b_xin.at[pl.ds(1, NX - 1)], bx_r)
-    for d in range(1, NX):
-        b_sum = b_sum + b_xin[d]
-    r_y[0] = a_sum
-    r_y[1] = b_sum
-    for d in AROUND_8:
-        send(r_y, r_yin.at[d], ry_s, ry_r, at_y(d))
-
-    arrive(g_xin.at[pl.ds(1, NX - 1)], gx_r)
-    for d in range(1, NX):
-        gram = gram + g_xin[d]
+        g_second = g_second + g_yin[1, d]
     rows_c = pl.ds(pl.multiple_of(RANK // 2 * c, RANK // 2), RANK // 2)
     rows_o = pl.ds(pl.multiple_of(RANK // 2 * o, RANK // 2), RANK // 2)
-    g_all[rows_c, :] = gram
+    g_all[rows_c, :] = jnp.concatenate([g_first, g_second], axis=0)
     send(g_all.at[rows_c], g_all.at[rows_c], gc_s, gc_r, sibling)
+    end_a(0)
+    end_a(1)
+    end_b(1)
+
     arrive(g_all.at[rows_o], gc_r)
-    inverse = invert_steps(g_all[...], 10)
-
-    term = r_y[...]
-    arrive(r_yin.at[pl.ds(1, NY - 1)], ry_r)
-    for d in range(1, NY):
-        term = term + r_yin[d]
-    r_all[:, rank_of(0), :] = term
-    for d in AROUND_4:
-        send(r_all.at[:, rank_of(0)], r_all.at[:, rank_of(0)], ra_s, ra_r, at_x(d))
-    inverse = invert_steps(inverse, 6)
+    inverse = invert_steps(g_all[...], 16)
+
+    for u in (2, 0, 1, 3):
+        arrive(r_yin.at[u, others_y], ry_r.at[u])
+        total = r_y[u]
+        for d in range(1, NY):
+            total = total + r_yin[u, d]
+        here = r_all.at[u // 2, pl.ds(pl.multiple_of(SLICE * x + PART * (u % 2), PART), PART)]
+        here[...] = total
+        for d in AROUND_4:
+            send(here, here, ra_s, ra_r, at_x(d))
     ortho_out[...] = dot(l_all[...], inverse, HIGHEST) * (1.0 / 16.0)
 
     @pl.when(mine)
@@ -285,24 +333,34 @@
     sent(others, la_s)
     sent(l_half, lf_s)
     sent(a_b16.at[pl.ds(0, 2 * (NX - 1))], ax_s)
-    sent(a_z.at[pl.ds(0, NZ - 1)], az_s)
-    sent(b_b16.at[pl.ds(0, NZ - 1)], bz_s)
-    sent(b_x.at[pl.ds(0, (NX - 1) * SLICE)], bx_s)
-    sent(r_yin.at[pl.ds(0, NY - 1)], ry_s)
-    sent(g_yin.at[pl.ds(0, NY - 1)], gy_s)
-    sent(g_xin.at[pl.ds(0, NX - 1)], gx_s)
-    sent(g_x, gc_s)
-    arrive(r_yin.at[pl.ds(0, NX - 1)], ra_r)
-    sent(r_yin.at[pl.ds(0, NX - 1)], ra_s)
-
-
-def update(ortho, right, params, momentum, new_params, new_momentum):
-    for h in range(2):
-        cols = slice(h * RANK, (h + 1) * RANK)
-        grad = dot(ortho[...], right[h], HIGHEST)
-        updated = outer_decay * momentum[:, cols] + grad
-        new_momentum[:, cols] = updated
-        new_params[:, cols] = params[:, cols] - outer_rate * (grad + outer_decay * updated)
+    sent(a_z.at[:, others_z], az_s)
+    sent(b_b16.at[:, others_z], bz_s)
+    sent(b_x.at[:, others_x], bx_s)
+    sent(r_yin.at[:, others_y], ry_s)
+    sent(g_yin.at[:, others_y], gy_s)
+    sent(g_xin.at[:, others_x], gx_s)
+    sent(g_own, gc_s)
+    right_others = r_yin.at[:, others_x]
+    arrive(right_others, ra_r)
+    sent(right_others, ra_s)
+
+
+def update(ortho, right, params, momentum, new_params, new_momentum, p_v, m_v, sem):
+    stores = []
+    for n in range(ROWS // STRIP):
+        rows = slice(n * STRIP, (n + 1) * STRIP)
+        for h in range(2):
+            cols = slice(h * RANK, (h + 1) * RANK)
+            grad = dot(ortho[rows, :], right[h], HIGHEST)
+            updated = outer_decay * momentum[rows, cols] + grad
+            m_v[rows, cols] = updated
+            p_v[rows, cols] = params[rows, cols] - outer_rate * (grad + outer_decay * updated)
+        for k, (src, dst) in enumerate(((m_v, new_momentum), (p_v, new_params))):
+            copy = pltpu.make_async_copy(src.at[rows], dst.at[rows], sem.at[n, k])
+            copy.start()
+            stores.append(copy)
+    for copy in stores:
+        copy.wait()
 
 
 def body(island_deltas, start_basis, outer_params, momentum):
@@ -321,19 +379,19 @@
         vmem((NZ, RANK, RANK), F32),
         vmem((NZ, RANK, RANK), BF16),
         vmem((NX, NZ, SLICE, RANK), BF16),
-        vmem((NZ, SLICE, RANK), F32),
-        vmem((NZ, SLICE, RANK), F32),
-        vmem((RANK, RANK), F32),
-        vmem((NZ, RANK, RANK), BF16),
-        vmem((NZ, RANK, RANK), BF16),
-        vmem((RANK, RANK), F32),
-        vmem((NX, SLICE, RANK), F32),
-        vmem((2, SLICE, RANK), F32),
-        vmem((NY, 2, SLICE, RANK), F32),
+        vmem((2, NZ, PART, RANK), F32),
+        vmem((2, NZ, PART, RANK), F32),
+        vmem((2, NX, PART, RANK), F32),
+        vmem((2, NZ, NX, PART, RANK), BF16),
+        vmem((2, NZ, NX, PART, RANK), BF16),
+        vmem((2, NX, PART, RANK), F32),
+        vmem((2, NX, PART, RANK), F32),
+        vmem((4, PART, RANK), F32),
+        vmem((4, NY, PART, RANK), F32),
         vmem((RANK // 2, RANK), F32),
-        vmem((NY, RANK // 2, RANK), F32),
-        vmem((RANK // 2, RANK), F32),
-        vmem((NX, RANK // 2, RANK), F32),
+        vmem((2, NY, RANK // 4, RANK), F32),
+        vmem((2, NX, RANK // 4, RANK), F32),
+        vmem((2, RANK // 4, RANK), F32),
         vmem((RANK, RANK), F32),
         *[dma(())] * 2,
         *[dma(())] * 2,
@@ -344,7 +402,11 @@
         *[dma(())] * 8,
         dma(()),
         dma((2,)),
-        *[dma(())] * 16,
+        *[dma(()), dma((2,))] * 3,
+        *[dma(()), dma((4,))],
+        *[dma(())] * 2,
+        *[dma(()), dma((2,))] * 2,
+        *[dma(())] * 2,
     ]
     in_vmem = pl.BlockSpec(memory_space=pltpu.VMEM)
     ortho, right = pl.pallas_call(
@@ -368,7 +430,8 @@
             name="update",
             out_shape=(state, state),
             in_specs=[in_vmem] * 4,
-            out_specs=(in_vmem, in_vmem),
+            out_specs=(pl.BlockSpec(memory_space=pl.ANY),) * 2,
+            scratch_shapes=[vmem((ROWS, BLOCK), F32), vmem((ROWS, BLOCK), F32), dma((ROWS // STRIP, 2))],
             compiler_params=pltpu.CompilerParams(vmem_limit_bytes=8 * 1024 * 1024),
         )(ortho, right, outer_params, momentum)
     )

time: 65.2 us -> 63 us (0.966); the launches traced: 65 us -> 62 us
  Pallas kernels: 64.3 us -> 61.3 us
    pallas_call x1, Pallas kernels: 62.9 us -> 60 us  [body(): pl.pallas_call(kernel, name='factors', out_shape=(jax.ShapeDtypeStruct((R...]
where the time goes in v5:
time: 63 us; the launch traced here: 62 us
  Pallas kernels  61.3 us (97%)
  between operations  0.67 us (1%)
    pallas_call x1, Pallas kernels, body(): pl.pallas_call(kernel, name='factors', out_shape=(jax.ShapeDtypeStruct((R...  60 us

profile of v5, /device:TPU:1, one launch (start us, length us, event | category | flops | bytes accessed | tf_op | source)
XLA Modules:
  0.0 62.0 jit_solution(13762931840834752646)
XLA Ops:
  0.6 0.0 copy-start.1
  0.6 0.0 copy-start
  0.7 60.0 %factors.1 = (f32[384,128]{1,0:T(8,128)S(1)}, f32[2,128,128]{2,1,0:T(8,128)S(1)}) custom-call(bf16[1,384,4096]{2,1,0:T(8,128)(2,1)} %deltas.1, bf16[128,128]{1,0:T(8,128)(2,1)} %basis.1), custom_call_target="tpu_custom_call" | custom-call | tf_op jit(solution)/shard_map/factors/pallas_call | solution.py:412
  60.7 0.0 copy-done.1
  60.7 0.0 copy-done
  60.7 1.3 %update.1 = (f32[384,256]{1,0:T(8,128)}, f32[384,256]{1,0:T(8,128)}) custom-call(f32[384,128]{1,0:T(8,128)S(1)} %get-tuple-element.4.ortho, f32[2,128,128]{2,1,0:T(8,128)S(1)} %get-tuple-element.5.right, f32[384,256]{1,0:T(8,128)S(1)} %copy-done, f32[384,256]{1,0:T(8,128)S(1)} %copy-done.1), custom_call_target="tpu_custom_call" | custom-call | tf_op jit(solution)/shard_map/update/pallas_call | solution.py:428
Async XLA Ops:
  0.6 60.1 %copy-start.1 = (f32[384,256]{1,0:T(8,128)S(1)}, f32[384,256]{1,0:T(8,128)}, u32[]{:S(2)}) copy-start(f32[384,256]{1,0:T(8,128)} %momentum.1) | copy-start | bytes 1179652
  0.6 60.1 %copy-start = (f32[384,256]{1,0:T(8,128)S(1)}, f32[384,256]{1,0:T(8,128)}, u32[]{:S(2)}) copy-start(f32[384,256]{1,0:T(8,128)} %params.1) | copy-start | bytes 1179652

commit v6 on v5

--- a/solution.py
+++ b/solution.py
@@ -28,7 +28,7 @@
 
 
 AROUND_8 = (4, 3, 5, 2, 6, 1, 7)
-AROUND_4 = (2, 1, 3)
+AROUND_4 = (1, 3, 2)
 
 
 def dot(a, b, precision=None):
@@ -129,7 +129,9 @@
     @pl.when(mine)
     def _():
         for d in (1, 7, 4, 2, 6, 3, 5):
-            send(basis_v, slot(own_slot), sy_s, sy_r.at[own_slot - 4 * x], at_y(d))
+            for t in range(2):
+                here = slot(own_slot).at[pl.ds(SHARD // 2 * t, SHARD // 2)]
+                send(basis_v.at[pl.ds(SHARD // 2 * t, SHARD // 2)], here, sy_s, sy_r.at[own_slot - 4 * x, t], at_y(d))
         slot(own_slot)[...] = basis_v[...]
 
     for b in range(NZ):
@@ -141,15 +143,17 @@
     for n, offset in enumerate(order):
         source = lax.rem(y + offset + NY, NY)
         k = lax.rem(source, 2) + 2 * (source // 4)
-        if n == 0:
-
-            @pl.when(jnp.logical_not(mine))
-            def _():
-                arrive(slot(4 * x + k), sy_r.at[k])
-        else:
-            arrive(slot(4 * x + k), sy_r.at[k])
-        for d in AROUND_4:
-            send(slot(4 * x + k), slot(4 * x + k), sx_s, sx_r.at[d - 1], at_x(d))
+        for t in range(2):
+            here = slot(4 * x + k).at[pl.ds(SHARD // 2 * t, SHARD // 2)]
+            if n == 0:
+
+                @pl.when(jnp.logical_not(mine))
+                def _():
+                    arrive(here, sy_r.at[k, t])
+            else:
+                arrive(here, sy_r.at[k, t])
+            for d in AROUND_4:
+                send(here, here, sx_s, sx_r.at[d - 1], at_x(d))
 
     pltpu.make_async_copy(d_own, d_own, load_sem).wait()
     arrive(d_sib, ds_r)
@@ -189,8 +193,7 @@
     left = l_all[...]
     left_t = left.T
 
-    g_part = dot(left_t, left, HIGHEST)
-    g_own[...] = jnp.where(c == 0, g_part[: RANK // 2], g_part[RANK // 2 :])
+    g_own[...] = dot(jnp.where(c == 0, left_t[: RANK // 2], left_t[RANK // 2 :]), left, HIGHEST)
     first, second = pl.ds(0, RANK // 4), pl.ds(RANK // 4, RANK // 4)
     for d in AROUND_8:
         send(g_own.at[first], g_yin.at[0, d], gy_s, gy_r.at[0], at_y(d))
@@ -294,6 +297,7 @@
         send(g_sum.at[0], g_xin.at[0, d], gx_s, gx_r.at[0], at_x(d))
     sum_b(1)
     end_b(0)
+    end_a(0)
     arrive(g_xin.at[0, others_x], gx_r.at[0])
     for d in range(1, NX):
         g_first = g_first + g_xin[0, d]
@@ -304,7 +308,6 @@
     rows_o = pl.ds(pl.multiple_of(RANK // 2 * o, RANK // 2), RANK // 2)
     g_all[rows_c, :] = jnp.concatenate([g_first, g_second], axis=0)
     send(g_all.at[rows_c], g_all.at[rows_c], gc_s, gc_r, sibling)
-    end_a(0)
     end_a(1)
     end_b(1)
 
@@ -396,7 +399,7 @@
         *[dma(())] * 2,
         *[dma(())] * 2,
         dma(()),
-        dma((4,)),
+        dma((4, 2)),
         dma(()),
         dma((NX - 1,)),
         *[dma(())] * 8,

time: 63 us -> 62.5 us (level)
  no operation moved by 1% of the time
where the time goes in v6:
time: 62.5 us; the launch traced here: 61.7 us
  Pallas kernels  61 us (98%)
  between operations  0.67 us (1%)
    pallas_call x1, Pallas kernels, body(): pl.pallas_call(kernel, name='factors', out_shape=(jax.ShapeDtypeStruct((R...  59.8 us
    pallas_call x1, Pallas kernels, body(): pl.pallas_call(update, name='update', out_shape=(state, state), in_specs=...  1.25 us

profile of v6, /device:TPU:1, one launch (start us, length us, event | category | flops | bytes accessed | tf_op | source)
XLA Modules:
  0.0 61.7 jit_solution(1277312791799435602)
XLA Ops:
  0.6 0.0 copy-start.1
  0.6 0.0 copy-start
  0.7 59.8 %factors.1 = (f32[384,128]{1,0:T(8,128)S(1)}, f32[2,128,128]{2,1,0:T(8,128)S(1)}) custom-call(bf16[1,384,4096]{2,1,0:T(8,128)(2,1)} %deltas.1, bf16[128,128]{1,0:T(8,128)(2,1)} %basis.1), custom_call_target="tpu_custom_call" | custom-call | tf_op jit(solution)/shard_map/factors/pallas_call | solution.py:415
  60.4 0.0 copy-done.1
  60.5 0.0 copy-done
  60.5 1.3 %update.1 = (f32[384,256]{1,0:T(8,128)}, f32[384,256]{1,0:T(8,128)}) custom-call(f32[384,128]{1,0:T(8,128)S(1)} %get-tuple-element.4.ortho, f32[2,128,128]{2,1,0:T(8,128)S(1)} %get-tuple-element.5.right, f32[384,256]{1,0:T(8,128)S(1)} %copy-done, f32[384,256]{1,0:T(8,128)S(1)} %copy-done.1), custom_call_target="tpu_custom_call" | custom-call | tf_op jit(solution)/shard_map/update/pallas_call | solution.py:431
Async XLA Ops:
  0.6 59.8 %copy-start.1 = (f32[384,256]{1,0:T(8,128)S(1)}, f32[384,256]{1,0:T(8,128)}, u32[]{:S(2)}) copy-start(f32[384,256]{1,0:T(8,128)} %momentum.1) | copy-start | bytes 1179652
  0.6 59.8 %copy-start = (f32[384,256]{1,0:T(8,128)S(1)}, f32[384,256]{1,0:T(8,128)}, u32[]{:S(2)}) copy-start(f32[384,256]{1,0:T(8,128)} %params.1) | copy-start | bytes 1179652

commit v7 on v6

--- a/solution.py
+++ b/solution.py
@@ -277,7 +277,10 @@
         for n in range(NZ - 1):
             total = total + a_zin[q, n]
         r_y[q] = total
-        send_y(q)
+        if q == 1:
+            both_q = pl.ds(0, 2)
+            for d in AROUND_8:
+                send(r_y.at[both_q], r_yin.at[both_q, d], ry_s, ry_r.at[0], at_y(d))
 
     def end_b(q):
         arrive(b_xin.at[q, others_x], bx_r.at[q])
@@ -315,7 +318,10 @@
     inverse = invert_steps(g_all[...], 16)
 
     for u in (2, 0, 1, 3):
-        arrive(r_yin.at[u, others_y], ry_r.at[u])
+        if u == 0:
+            arrive(r_yin.at[pl.ds(0, 2), others_y], ry_r.at[0])
+        elif u > 1:
+            arrive(r_yin.at[u, others_y], ry_r.at[u])
         total = r_y[u]
         for d in range(1, NY):
             total = total + r_yin[u, d]

time: 62.5 us -> 63.3 us (1.013)
  no operation moved by 1% of the time
where the time goes in v7:
time: 63.3 us; the launch traced here: 62.3 us
  Pallas kernels  61.6 us (97%)
  between operations  0.67 us (1%)
    pallas_call x1, Pallas kernels, body(): pl.pallas_call(kernel, name='factors', out_shape=(jax.ShapeDtypeStruct((R...  60.4 us

profile of v7, /device:TPU:1, one launch (start us, length us, event | category | flops | bytes accessed | tf_op | source)
XLA Modules:
  0.0 62.3 jit_solution(6956169953479356858)
XLA Ops:
  0.6 0.0 copy-start.1
  0.6 0.0 copy-start
  0.7 60.4 %factors.1 = (f32[384,128]{1,0:T(8,128)S(1)}, f32[2,128,128]{2,1,0:T(8,128)S(1)}) custom-call(bf16[1,384,4096]{2,1,0:T(8,128)(2,1)} %deltas.1, bf16[128,128]{1,0:T(8,128)(2,1)} %basis.1), custom_call_target="tpu_custom_call" | custom-call | tf_op jit(solution)/shard_map/factors/pallas_call | solution.py:421
  61.0 0.0 copy-done.1
  61.0 0.0 copy-done
  61.0 1.3 %update.1 = (f32[384,256]{1,0:T(8,128)}, f32[384,256]{1,0:T(8,128)}) custom-call(f32[384,128]{1,0:T(8,128)S(1)} %get-tuple-element.4.ortho, f32[2,128,128]{2,1,0:T(8,128)S(1)} %get-tuple-element.5.right, f32[384,256]{1,0:T(8,128)S(1)} %copy-done, f32[384,256]{1,0:T(8,128)S(1)} %copy-done.1), custom_call_target="tpu_custom_call" | custom-call | tf_op jit(solution)/shard_map/update/pallas_call | solution.py:437
Async XLA Ops:
  0.6 60.4 %copy-start.1 = (f32[384,256]{1,0:T(8,128)S(1)}, f32[384,256]{1,0:T(8,128)}, u32[]{:S(2)}) copy-start(f32[384,256]{1,0:T(8,128)} %momentum.1) | copy-start | bytes 1179652
  0.6 60.4 %copy-start = (f32[384,256]{1,0:T(8,128)S(1)}, f32[384,256]{1,0:T(8,128)}, u32[]{:S(2)}) copy-start(f32[384,256]{1,0:T(8,128)} %params.1) | copy-start | bytes 1179652
